TPU v7x, 256 devices: a whole 4x4x8 slice. The times are simulated.
256 devices in a mesh: gz: 32 (over y_lo, z, core), gy: 8 (over x, y_hi).
Axes of the slice: x: 4, y: 4 (y_hi: 2, y_lo: 2; y = y_hi * 2 + y_lo), z: 8, core: 2. Of those that a mesh axis runs over, the one named last changes fastest.
Arguments:
- potential: float32 [256, 512, 512], P('gz', 'gy'), may hold values from 0 to 1
- fast_gate: float32 [256, 512, 512], P('gz', 'gy'), may hold values from 0 to 1
- slow_gate: float32 [256, 512, 512], P('gz', 'gy'), may hold values from 0 to 1
- tissue: int32 [256, 512, 512], P('gz', 'gy'), may hold values 0 or 1
- region_ids: int32 [32, 64, 64], P('gz', 'gy'), may hold values from 0 to 7
- fibre_table: float32 [8, 3], replicated, may hold values from -1 to 1
- inverse_x: float32 [512, 512], replicated, may hold values from -1 to 1
- inverse_z: float32 [256, 256], replicated, may hold values from -1 to 1
- inverse_y: float32 [512, 512], replicated, may hold values from -1 to 1
Outputs:
- new_potential: float32 [256, 512, 512], P('gz', 'gy')
- new_fast: float32 [256, 512, 512], P('gz', 'gy')
- new_slow: float32 [256, 512, 512], P('gz', 'gy')
All inputs are finite; a program needn't handle non-finite values. No bound on the sum of `tissue` on one device may be relied on, other than what follows from the above.
Results may differ from a plain program's by a relative error of at most 0.0003.
Values sent between devices are 32-bit elements; how exact they have to be, the bound alone decides.
No kernel may reach another device: no remote copies, remote signals or barrier semaphores. Data moves between devices by JAX's collectives and lax.ppermute only.
A program may use at most 64 MiB of HBM per device.

v0:
```python
import jax
import jax.numpy as jnp
from jax import lax
from jax.sharding import PartitionSpec as P

time_step = 0.1
depol_tau = 0.25
repol_tau = 33.33
inward_tau = 29.0
outward_tau = 12.5
vclose_tau = 3.33
vopen_high = 19.6
vopen_low = 1250.0
wclose_tau = 870.0
wopen_tau = 41.0
gate_crit = 0.13
vgate_crit = 0.04
inward_crit = 0.85
inward_slope = 10.0


def with_halo(cells, sides, width):
    for axis, dim in sides:
        count = lax.axis_size(axis)
        ends = count - 1
        head = lax.slice_in_dim(cells, 0, width, axis=dim)
        tail = lax.slice_in_dim(cells, cells.shape[dim] - width, cells.shape[dim], axis=dim)
        cells = jnp.concatenate(
            [
                lax.ppermute(tail, axis, [(i, (i + 1) % count) for i in range(ends)]),
                cells,
                lax.ppermute(head, axis, [((i + 1) % count, i) for i in range(ends)]),
            ],
            axis=dim,
        )
    return cells


def ionic(potential, fast_gate, slow_gate, tissue):
    active = potential >= gate_crit
    current = jnp.where(
        active, -fast_gate * (1.0 - potential) * (potential - gate_crit) / depol_tau, 0.0
    )
    current = current + jnp.where(active, 1.0 / repol_tau, potential / outward_tau)
    current = current - slow_gate * (1.0 + jnp.tanh(inward_slope * (potential - inward_crit))) / (
        2.0 * inward_tau
    )
    excited = potential - time_step * current
    target = jnp.where(active, 0.0, 1.0)
    tau_fast = jnp.where(
        active, vclose_tau, jnp.where(potential >= vgate_crit, vopen_high, vopen_low)
    )
    tau_slow = jnp.where(active, wclose_tau, wopen_tau)
    new_fast = target + (fast_gate - target) * jnp.exp(-time_step / tau_fast)
    new_slow = target + (slow_gate - target) * jnp.exp(-time_step / tau_slow)
    living = tissue == 1
    return (
        jnp.where(living, excited, potential),
        jnp.where(living, new_fast, fast_gate),
        jnp.where(living, new_slow, slow_gate),
    )


def couplings(region_ids, fibre_table):
    picks = (region_ids[..., None] == jnp.arange(fibre_table.shape[0], dtype=jnp.int32)).astype(
        jnp.float32
    )
    return [jnp.sum(picks * fibre_table[:, column], axis=-1) for column in range(3)]


def blockwise(field, weight):
    za, ya, xa = weight.shape
    shaped = field.reshape(za, 8, ya, 8, xa, 8)
    return (shaped * weight[:, None, :, None, :, None]).reshape(field.shape)


def cross_term(padded, region_ids, fibre_table):
    mixed_xy = (
        padded[1:-1, 2:, 2:]
        - padded[1:-1, 2:, :-2]
        - padded[1:-1, :-2, 2:]
        + padded[1:-1, :-2, :-2]
    ) / 4.0
    mixed_xz = (
        padded[2:, 1:-1, 2:]
        - padded[2:, 1:-1, :-2]
        - padded[:-2, 1:-1, 2:]
        + padded[:-2, 1:-1, :-2]
    ) / 4.0
    mixed_yz = (
        padded[2:, 2:, 1:-1]
        - padded[2:, :-2, 1:-1]
        - padded[:-2, 2:, 1:-1]
        + padded[:-2, :-2, 1:-1]
    ) / 4.0
    coef_xy, coef_xz, coef_yz = couplings(region_ids, fibre_table)
    total = (
        blockwise(mixed_xy, coef_xy) + blockwise(mixed_xz, coef_xz) + blockwise(mixed_yz, coef_yz)
    )
    return 2.0 * total


def shards(
    potential,
    fast_gate,
    slow_gate,
    tissue,
    region_ids,
    fibre_table,
    inverse_x,
    inverse_z,
    inverse_y,
):
    bordered = with_halo(potential, (("gz", 0), ("gy", 1)), 1)
    bordered = jnp.pad(bordered, ((0, 0), (0, 0), (1, 1)))
    excited, new_fast, new_slow = ionic(potential, fast_gate, slow_gate, tissue)
    rhs = excited + cross_term(bordered, region_ids, fibre_table)
    along_x = jnp.einsum("zyj,ij->zyi", rhs, inverse_x, precision=lax.Precision.HIGHEST)
    along_z = jnp.einsum(
        "ij,jyx->iyx",
        inverse_z,
        lax.all_to_all(along_x, "gz", split_axis=1, concat_axis=0, tiled=True),
        precision=lax.Precision.HIGHEST,
    )
    restored = lax.all_to_all(along_z, "gz", split_axis=0, concat_axis=1, tiled=True)
    y_blocks = lax.all_to_all(restored, "gy", split_axis=0, concat_axis=1, tiled=True)
    solved = jnp.einsum("ij,zjx->zix", inverse_y, y_blocks, precision=lax.Precision.HIGHEST)
    new_potential = lax.all_to_all(solved, "gy", split_axis=1, concat_axis=0, tiled=True)
    return (new_potential, new_fast, new_slow)


def solution(mesh):
    return jax.shard_map(
        shards,
        mesh=mesh,
        in_specs=(
            P("gz", "gy", None),
            P("gz", "gy", None),
            P("gz", "gy", None),
            P("gz", "gy", None),
            P("gz", "gy", None),
            P(),
            P(),
            P(),
            P(),
        ),
        out_specs=(P("gz", "gy", None), P("gz", "gy", None), P("gz", "gy", None)),
        check_vma=False,
    )
```

profile of v0, /device:TPU:32, one launch (start us, length us, event | category | flops | bytes accessed | tf_op | source)
XLA Modules:
  0.0 164.3 jit_solution(7557296398678198246)
XLA Ops:
  0.6 1.1 fusion.24
  1.7 1.9 %collective-permute-start.1 = (f32[1,64,512]{2,1,0:T(8,128)S(1)}, f32[1,64,512]{2,1,0:T(8,128)S(1)}, u32[]{:S(2)}, u32[]{:S(2)}) collective-permute-start(f32[1,64,512]{2,1,0:T(8,128)S(1)} %get-tuple-element.15), channel_id=1, source_target_pairs={{8,0},{16,8},{24,16},{32,24},{40,32},{48,40},{56,48},{64,56},{72,6... | collective-permute-start | bytes 393224 | tf_op jit(solution)/shard_map/ppermute | solution.py:32
  3.7 2.4 %collective-permute-start = (f32[1,64,512]{2,1,0:T(8,128)S(1)}, f32[1,64,512]{2,1,0:T(8,128)S(1)}, u32[]{:S(2)}, u32[]{:S(2)}) collective-permute-start(f32[1,64,512]{2,1,0:T(8,128)S(1)} %get-tuple-element.16), channel_id=1, source_target_pairs={{0,8},{8,16},{16,24},{24,32},{32,40},{40,48},{48,56},{56,64},{64,7... | collective-permute-start | bytes 393224 | tf_op jit(solution)/shard_map/ppermute | solution.py:30
  6.1 0.8 slice_bitcast_fusion.1
  6.9 3.5 %fusion.13 = (f32[8,64,512]{2,1,0:T(8,128)}, pred[8,64,512]{2,1,0:T(8,128)(4,1)S(1)}) fusion(f32[8,64,512]{2,1,0:T(8,128)} %param.11, f32[8,64,512]{2,1,0:T(8,128)} %param.9, s32[8,64,512]{2,1,0:T(8,128)} %param.12), kind=kLoop, calls=%fused_computation.28 | loop fusion | flops 2359296 | bytes 4456448 | tf_op jit(solution)/shard_map/jit(_where)/select_n | solution.py:60
  10.5 1.5 fusion.11
  12.7 1.3 collective-permute-start.3
  14.0 6.7 %collective-permute-start.2 = (f32[10,1,512]{2,1,0:T(1,128)}, f32[10,1,512]{2,1,0:T(1,128)}, u32[]{:S(2)}, u32[]{:S(2)}) collective-permute-start(f32[10,1,512]{2,1,0:T(1,128)} %get-tuple-element.12), channel_id=1, source_target_pairs={{0,1},{1,2},{2,3},{3,4},{4,5},{5,6},{6,7},{8,9},{9,10},{10,11},{11... | collective-permute-start | bytes 61448 | tf_op jit(solution)/shard_map/ppermute | solution.py:30
  20.7 1.7 %mul.144 = f32[8,8,64,8]{3,2,1,0:T(8,128)} broadcast(f32[8,64]{1,0:T(8,128)S(1)} %get-tuple-element.20), dimensions={0,2} | broadcast | bytes 133120 | tf_op jit(solution)/shard_map/mul | solution.py:74
  22.3 2.8 %mul.145 = f32[64,512]{1,0:T(8,128)S(1)} reshape(f32[8,8,64,8]{3,2,1,0:T(8,128)} %mul.144) | data formatting | bytes 262144 | tf_op jit(solution)/shard_map/mul | solution.py:74
  25.1 1.7 %mul.128 = f32[8,8,64,8]{3,2,1,0:T(8,128)} broadcast(f32[8,64]{1,0:T(8,128)S(1)} %broadcast_multiply_fusion.2), dimensions={0,2} | broadcast | bytes 133120 | tf_op jit(solution)/shard_map/mul | solution.py:74
  26.8 3.4 %mul.129 = f32[64,512]{1,0:T(8,128)} reshape(f32[8,8,64,8]{3,2,1,0:T(8,128)} %mul.128) | data formatting | bytes 262144 | tf_op jit(solution)/shard_map/mul | solution.py:74
  30.2 1.7 %mul.136 = f32[8,8,64,8]{3,2,1,0:T(8,128)} broadcast(f32[8,64]{1,0:T(8,128)S(1)} %get-tuple-element.21), dimensions={0,2} | broadcast | bytes 133120 | tf_op jit(solution)/shard_map/mul | solution.py:74
  31.8 3.4 %mul.137 = f32[64,512]{1,0:T(8,128)} reshape(f32[8,8,64,8]{3,2,1,0:T(8,128)} %mul.136) | data formatting | bytes 262144 | tf_op jit(solution)/shard_map/mul | solution.py:74
  35.3 1.6 select_maximum_fusion
  37.0 4.1 %fusion.8 = f32[8,64,512]{2,1,0:T(8,128)S(1)} fusion(f32[10,1,512]{2,1,0:T(1,128)} %collective-permute-done.2, f32[10,64,512]{2,1,0:T(8,128)S(1)} %constant_dynamic-update-slice_fusion, f32[10,1,512]{2,1,0:T(1,128)} %collective-permute-done.3, pred[8,64,512]{2,1,0:T(8,128)(4,1)S(1)} %copy-done.6, f32[8,64,512]{2,1,0:T(8,128)S(1)} %copy-done.1, ...), kind=kLoop, calls=%fused_computation.23 | loop fusion | flops 10485760 | bytes 14589952 | tf_op jit(solution)/shard_map/add | solution.py:117
  41.1 2.4 %fusion.18 = f32[8,64,512]{2,0,1:T(8,128)S(1)} fusion(f32[512,512]{1,0:T(8,128)S(1)} %copy-done, f32[8,64,512]{2,1,0:T(8,128)S(1)} %fusion.8), kind=kOutput, calls=%fused_computation.41 | convolution fusion | flops 1610612736 | bytes 3145728 | tf_op jit(solution)/shard_map/zyj,ij->zyi/dot_general | solution.py:118
  43.5 39.2 %all_to_all.57 = f32[8,64,512]{2,0,1:T(8,128)S(1)} all-to-all(f32[8,64,512]{2,0,1:T(8,128)S(1)} %fusion.18), channel_id=1, replica_groups=mesh['gz'=32,'gy'=8] {'gz'}, dimensions={1} | all-to-all | bytes 2097152 | tf_op jit(solution)/shard_map/all_to_all | solution.py:122
  82.7 1.8 %convolution_bitcast_fusion.1 = f32[256,2,512]{0,2,1:T(8,128)S(1)} fusion(f32[32,8,2,512]{3,1,2,0:T(8,128)S(1)} %bitcast.42, f32[256,256]{1,0:T(8,128)S(1)} %copy-done.10), kind=kOutput, calls=%fused_computation.15 | convolution fusion | flops 805306368 | bytes 2359296 | tf_op jit(solution)/shard_map/ij,jyx->iyx/dot_general | solution.py:119
  85.1 32.2 %all_to_all.58 = f32[256,2,512]{2,1,0:T(2,128)S(1)} all-to-all(f32[256,2,512]{2,1,0:T(2,128)S(1)} %copy.43), channel_id=1, replica_groups=mesh['gz'=32,'gy'=8] {'gz'}, dimensions={0} | all-to-all | bytes 2097152 | tf_op jit(solution)/shard_map/all_to_all | solution.py:125
  118.3 22.9 %all_to_all.59 = f32[8,64,512]{2,1,0:T(8,128)S(1)} all-to-all(f32[8,64,512]{2,1,0:T(8,128)S(1)} %copy.46), channel_id=1, replica_groups=mesh['gz'=32,'gy'=8] {'gy'}, dimensions={0} | all-to-all | bytes 2097152 | tf_op jit(solution)/shard_map/all_to_all | solution.py:126
  141.2 3.5 %convolution_bitcast_fusion = f32[1,512,512]{1,2,0:T(8,128)S(1)} fusion(f32[512,512]{1,0:T(8,128)S(1)} %bitcast.41, f32[512,512]{1,0:T(8,128)S(1)} %copy-done.7), kind=kOutput, calls=%fused_computation.14 | convolution fusion | flops 1610612736 | bytes 3145728 | tf_op jit(solution)/shard_map/ij,zjx->zix/dot_general | solution.py:127
  145.5 17.8 %all_to_all.60 = f32[1,512,512]{2,0,1:T(1,128)S(1)} all-to-all(f32[1,512,512]{2,0,1:T(1,128)S(1)} %copy.47), channel_id=1, replica_groups=mesh['gz'=32,'gy'=8] {'gy'}, dimensions={1} | all-to-all | bytes 2097152 | tf_op jit(solution)/shard_map/all_to_all | solution.py:128
  163.3 1.0 copy.51
  (39 shorter events, 3.1 us)
Async XLA Ops:
  0.6 40.5 %copy-start = (f32[512,512]{1,0:T(8,128)S(1)}, f32[512,512]{1,0:T(8,128)}, u32[]{:S(2)}) copy-start(f32[512,512]{1,0:T(8,128)} %param.15) | copy-start | bytes 3145732
  1.7 10.3 %collective-permute-start.1 = (f32[1,64,512]{2,1,0:T(8,128)S(1)}, f32[1,64,512]{2,1,0:T(8,128)S(1)}, u32[]{:S(2)}, u32[]{:S(2)}) collective-permute-start(f32[1,64,512]{2,1,0:T(8,128)S(1)} %get-tuple-element.15), channel_id=1, source_target_pairs={{8,0},{16,8},{24,16},{32,24},{40,32},{48,40},{56,48},{64,56},{72,6... | collective-permute-start | bytes 393224 | tf_op jit(solution)/shard_map/ppermute | solution.py:32
  3.7 6.8 %collective-permute-start = (f32[1,64,512]{2,1,0:T(8,128)S(1)}, f32[1,64,512]{2,1,0:T(8,128)S(1)}, u32[]{:S(2)}, u32[]{:S(2)}) collective-permute-start(f32[1,64,512]{2,1,0:T(8,128)S(1)} %get-tuple-element.16), channel_id=1, source_target_pairs={{0,8},{8,16},{16,24},{24,32},{32,40},{40,48},{48,56},{56,64},{64,7... | collective-permute-start | bytes 393224 | tf_op jit(solution)/shard_map/ppermute | solution.py:30
  6.9 3.5 %copy-start.11 = (s32[1,8,64]{2,1,0:T(8,128)S(1)}, s32[1,8,64]{2,1,0:T(8,128)}, u32[]{:S(2)}) copy-start(s32[1,8,64]{2,1,0:T(8,128)} %param.13) | copy-start | bytes 6148
  6.9 3.7 %copy-start.1 = (f32[8,64,512]{2,1,0:T(8,128)S(1)}, f32[8,64,512]{2,1,0:T(8,128)}, u32[]{:S(2)}) copy-start(f32[8,64,512]{2,1,0:T(8,128)} %param.9) | copy-start | bytes 3145732
  6.9 3.7 %copy-start.3 = (f32[8,64,512]{2,1,0:T(8,128)S(1)}, f32[8,64,512]{2,1,0:T(8,128)}, u32[]{:S(2)}) copy-start(f32[8,64,512]{2,1,0:T(8,128)} %param.10) | copy-start | bytes 3145732
  10.4 1.7 %copy-start.5 = (pred[8,64,512]{2,1,0:T(8,128)(4,1)}, pred[8,64,512]{2,1,0:T(8,128)(4,1)S(1)}, u32[]{:S(2)}) copy-start(pred[8,64,512]{2,1,0:T(8,128)(4,1)S(1)} %get-tuple-element.10) | copy-start | bytes 786436
  12.7 22.6 %collective-permute-start.3 = (f32[10,1,512]{2,1,0:T(1,128)}, f32[10,1,512]{2,1,0:T(1,128)}, u32[]{:S(2)}, u32[]{:S(2)}) collective-permute-start(f32[10,1,512]{2,1,0:T(1,128)} %get-tuple-element.11), channel_id=1, source_target_pairs={{1,0},{2,1},{3,2},{4,3},{5,4},{6,5},{7,6},{9,8},{10,9},{11,10},{12... | collective-permute-start | bytes 61448 | tf_op jit(solution)/shard_map/ppermute | solution.py:32
  14.0 21.3 %collective-permute-start.2 = (f32[10,1,512]{2,1,0:T(1,128)}, f32[10,1,512]{2,1,0:T(1,128)}, u32[]{:S(2)}, u32[]{:S(2)}) collective-permute-start(f32[10,1,512]{2,1,0:T(1,128)} %get-tuple-element.12), channel_id=1, source_target_pairs={{0,1},{1,2},{2,3},{3,4},{4,5},{5,6},{6,7},{8,9},{9,10},{10,11},{11... | collective-permute-start | bytes 61448 | tf_op jit(solution)/shard_map/ppermute | solution.py:30
  35.3 1.7 %copy-start.2 = (f32[8,64,512]{2,1,0:T(8,128)S(1)}, f32[8,64,512]{2,1,0:T(8,128)}, u32[]{:S(2)}) copy-start(f32[8,64,512]{2,1,0:T(8,128)} %param.11) | copy-start | bytes 3145732
  35.3 1.7 %copy-start.4 = (f32[8,64,512]{2,1,0:T(8,128)S(1)}, f32[8,64,512]{2,1,0:T(8,128)}, u32[]{:S(2)}) copy-start(f32[8,64,512]{2,1,0:T(8,128)} %param.10) | copy-start | bytes 3145732
  35.3 1.7 %copy-start.6 = (pred[8,64,512]{2,1,0:T(8,128)(4,1)S(1)}, pred[8,64,512]{2,1,0:T(8,128)(4,1)}, u32[]{:S(2)}) copy-start(pred[8,64,512]{2,1,0:T(8,128)(4,1)} %copy-done.5) | copy-start | bytes 786436
  35.3 1.7 %copy-start.8 = (f32[64,512]{1,0:T(8,128)S(1)}, f32[64,512]{1,0:T(8,128)}, u32[]{:S(2)}) copy-start(f32[64,512]{1,0:T(8,128)} %mul.129) | copy-start | bytes 393220
  35.3 1.7 %copy-start.9 = (f32[64,512]{1,0:T(8,128)S(1)}, f32[64,512]{1,0:T(8,128)}, u32[]{:S(2)}) copy-start(f32[64,512]{1,0:T(8,128)} %mul.137) | copy-start | bytes 393220
  41.1 41.6 %copy-start.10 = (f32[256,256]{1,0:T(8,128)S(1)}, f32[256,256]{1,0:T(8,128)}, u32[]{:S(2)}) copy-start(f32[256,256]{1,0:T(8,128)} %param.16) | copy-start | bytes 786436
  117.7 23.5 %copy-start.7 = (f32[512,512]{1,0:T(8,128)S(1)}, f32[512,512]{1,0:T(8,128)}, u32[]{:S(2)}) copy-start(f32[512,512]{1,0:T(8,128)} %param.17) | copy-start | bytes 3145732
where the time goes:
time: 165 us; the launch traced here: 164 us
  blocking collectives  112 us (68%)
  local copies, waits for them, and re-layouts  20.5 us (12%)
  starting transfers between devices  12.3 us (7%)
  other arithmetic  10.8 us (7%)
  matrix products  7.7 us (5%)
    all_to_all x1, blocking collectives, shards(): lax.all_to_all(along_x, 'gz', split_axis=1, concat_axis=0, tiled=True)  39.2 us
    all_to_all x1, blocking collectives, shards(): lax.all_to_all(along_z, 'gz', split_axis=0, concat_axis=1, tiled=True)  32.2 us
    all_to_all x1, blocking collectives, shards(): lax.all_to_all(restored, 'gy', split_axis=0, concat_axis=1, tiled=True)  22.9 us
    all_to_all x1, blocking collectives, shards(): lax.all_to_all(solved, 'gy', split_axis=1, concat_axis=0, tiled=True)  17.8 us
    mul x6, local copies, waits for them, and re-layouts, blockwise(): return (shaped * weight[:, None, :, None, :, None]).reshape(field.shape)  14.6 us
    ppermute x2, starting transfers between devices, with_halo(): lax.ppermute(tail, axis, [(i, (i + 1) % count) for i in range(ends)])  9.06 us
    add x1, other arithmetic, shards(): rhs = excited + cross_term(bordered, region_ids, fibre_table)  4.1 us
    select_n x1, other arithmetic, ionic(): jnp.where(living, new_slow, slow_gate)  3.5 us
  transfers between devices with their start and end apart: 4, of which 0 were waited for; matrix products, arithmetic and copies ran while one was open for 12% of the time, Pallas kernels for 0%

commit v1 on v0

v1 whole, which is shorter than its diff:
```python
import math

import jax
import jax.numpy as jnp
from jax import lax
from jax.experimental import pallas as pl
from jax.experimental.pallas import tpu as pltpu
from jax.sharding import PartitionSpec as P

time_step = 0.1
depol_tau = 0.25
repol_tau = 33.33
inward_tau = 29.0
outward_tau = 12.5
vclose_tau = 3.33
vopen_high = 19.6
vopen_low = 1250.0
wclose_tau = 870.0
wopen_tau = 41.0
gate_crit = 0.13
vgate_crit = 0.04
inward_crit = 0.85
inward_slope = 10.0

VMEM = pl.BlockSpec(memory_space=pltpu.VMEM)
SMEM = pl.BlockSpec(memory_space=pltpu.SMEM)
NT = (((1,), (1,)), ((), ()))
NN = (((1,), (0,)), ((), ()))


def decay(tau):
    return math.exp(-time_step / tau)


def split(values):
    high = values.astype(jnp.bfloat16)
    return high, (values - high.astype(jnp.float32)).astype(jnp.bfloat16)


def product(left, right, dims):
    (lh, ll), (rh, rl) = left, right

    def dot(a, b):
        return lax.dot_general(a, b, dims, preferred_element_type=jnp.float32)

    return dot(lh, rh) + (dot(lh, rl) + dot(ll, rh))


def ionic_kernel(pot_ref, fast_ref, slow_ref, tissue_ref, exc_ref, nfast_ref, nslow_ref):
    p, v, w = pot_ref[...], fast_ref[...], slow_ref[...]
    living = tissue_ref[...] == 1
    active = p >= gate_crit
    current = jnp.where(
        active,
        (1.0 / repol_tau) - v * (1.0 - p) * (p - gate_crit) * (1.0 / depol_tau),
        p * (1.0 / outward_tau),
    )
    current = current - w * (1.0 + jnp.tanh(inward_slope * (p - inward_crit))) * (
        1.0 / (2.0 * inward_tau)
    )
    exc_ref[...] = jnp.where(living, p - time_step * current, p)
    target = jnp.where(active, 0.0, 1.0)
    keep_fast = jnp.where(
        active, decay(vclose_tau), jnp.where(p >= vgate_crit, decay(vopen_high), decay(vopen_low))
    )
    keep_slow = jnp.where(active, decay(wclose_tau), decay(wopen_tau))
    nfast_ref[...] = jnp.where(living, target + (v - target) * keep_fast, v)
    nslow_ref[...] = jnp.where(living, target + (w - target) * keep_slow, w)


def ionic(potential, fast_gate, slow_gate, tissue):
    nz, ny, nx = potential.shape
    block = pl.BlockSpec((1, ny, nx), lambda z: (z, 0, 0))
    shape = jax.ShapeDtypeStruct((nz, ny, nx), jnp.float32)
    return pl.pallas_call(
        ionic_kernel,
        grid=(nz,),
        in_specs=[block] * 4,
        out_specs=[block] * 3,
        out_shape=[shape] * 3,
        cost_estimate=pl.CostEstimate(
            flops=40 * nz * ny * nx, bytes_accessed=28 * nz * ny * nx, transcendentals=0
        ),
        name="ionic",
    )(potential, fast_gate, slow_gate, tissue)


def lane_difference(values):
    width = values.shape[-1]
    lane = lax.broadcasted_iota(jnp.int32, values.shape, values.ndim - 1)
    ahead = pltpu.roll(values, width - 1, values.ndim - 1)
    behind = pltpu.roll(values, 1, values.ndim - 1)
    return jnp.where(lane == width - 1, 0.0, ahead) - jnp.where(lane == 0, 0.0, behind)


def cross_kernel(
    table_ref, pot_ref, exc_ref, zlo_ref, zhi_ref, ylo_ref, yhi_ref, region_ref, inv_ref,
    out_ref, pad_ref, dy_ref, coef_ref, high_ref, low_ref,
):
    nz, ny, nx = pot_ref.shape
    blocks = nx // 8
    regions = table_ref.shape[0]
    spread = (
        lax.broadcasted_iota(jnp.int32, (blocks, nx), 1) // 8
        == lax.broadcasted_iota(jnp.int32, (blocks, nx), 0)
    ).astype(jnp.bfloat16)
    ids = lax.dot_general(
        region_ref[...].astype(jnp.float32).astype(jnp.bfloat16), spread, NN,
        preferred_element_type=jnp.float32,
    )
    for column in range(3):
        coef = jnp.zeros_like(ids)
        for region in range(regions):
            coef = jnp.where(ids == float(region), 0.5 * table_ref[region, column], coef)
        coef_ref[column] = coef

    for z in range(nz + 2):
        plane = zlo_ref[...] if z == 0 else zhi_ref[...] if z == nz + 1 else pot_ref[z - 1]
        pad_ref[z, 8 : 8 + ny] = plane
        pad_ref[z, 7:8] = ylo_ref[z : z + 1]
        pad_ref[z, 8 + ny : 9 + ny] = yhi_ref[z : z + 1]
        dy_ref[z] = pad_ref[z, 9 : 9 + ny] - pad_ref[z, 7 : 7 + ny]

    for z in range(nz):
        mixed_xy = lane_difference(dy_ref[z + 1])
        mixed_xz = lane_difference(pad_ref[z + 2, 8 : 8 + ny] - pad_ref[z, 8 : 8 + ny])
        mixed_yz = dy_ref[z + 2] - dy_ref[z]
        for b in range(ny // 8):
            rows = slice(8 * b, 8 * b + 8)
            rhs = exc_ref[z, rows] + (
                coef_ref[0, b : b + 1] * mixed_xy[rows]
                + coef_ref[1, b : b + 1] * mixed_xz[rows]
                + coef_ref[2, b : b + 1] * mixed_yz[rows]
            )
            pad_ref[0, rows] = rhs
        high, low = split(pad_ref[0, 0:ny])
        high_ref[z * ny : (z + 1) * ny] = high
        low_ref[z * ny : (z + 1) * ny] = low

    half = nx // 2
    matrix = split(inv_ref[...])
    first = lax.broadcasted_iota(jnp.int32, (half, 2 * ny), 1) < ny
    for z in range(0, nz, 2):
        rows = slice(z * ny, (z + 2) * ny)
        solved = product(matrix, (high_ref[rows], low_ref[rows]), NT)
        lower, upper = solved[:half], solved[half:]
        out_ref[:, z, :] = jnp.where(first, lower, pltpu.roll(upper, ny, 1))
        out_ref[:, z + 1, :] = jnp.where(first, pltpu.roll(lower, ny, 1), upper)


def cross_solve(table, potential, excited, zlo, zhi, ylo, yhi, region, inverse_x):
    nz, ny, nx = potential.shape
    return pl.pallas_call(
        cross_kernel,
        in_specs=[SMEM] + [VMEM] * 8,
        out_specs=VMEM,
        out_shape=jax.ShapeDtypeStruct((nx // 2, nz, 2 * ny), jnp.float32),
        scratch_shapes=[
            pltpu.VMEM((nz + 2, ny + 16, nx), jnp.float32),
            pltpu.VMEM((nz + 2, ny, nx), jnp.float32),
            pltpu.VMEM((3, ny // 8, nx), jnp.float32),
            pltpu.VMEM((nz * ny, nx), jnp.bfloat16),
            pltpu.VMEM((nz * ny, nx), jnp.bfloat16),
        ],
        compiler_params=pltpu.CompilerParams(vmem_limit_bytes=40 * 1024 * 1024),
        cost_estimate=pl.CostEstimate(
            flops=6 * nz * ny * nx * nx, bytes_accessed=16 * nz * ny * nx, transcendentals=0
        ),
        name="cross_solve",
    )(table, potential, excited, zlo, zhi, ylo, yhi, region, inverse_x)


def plane_kernel(in_ref, invz_ref, invy_ref, out_ref, high_ref, low_ref):
    slabs, blocks, depth, width = in_ref.shape
    half = width // 2
    rows = slabs * depth
    matz, maty = split(invz_ref[...]), split(invy_ref[...])
    first = lax.broadcasted_iota(jnp.int32, (rows, width), 1) < half
    for b in range(0, blocks, 2):
        pair = []
        for k in (b, b + 1):
            pair.append(in_ref[:, k].reshape(rows, width))
        solved = product(matz, split(jnp.concatenate(pair, axis=1)), NN)
        left, right = solved[:, :width], solved[:, width:]
        columns = slice(b * half, (b + 2) * half)
        high_ref[:rows, columns], low_ref[:rows, columns] = split(
            jnp.where(first, left, pltpu.roll(right, half, 1))
        )
        high_ref[rows:, columns], low_ref[rows:, columns] = split(
            jnp.where(first, pltpu.roll(left, half, 1), right)
        )
    for b in range(0, blocks, 2):
        columns = slice(b * half, (b + 2) * half)
        solved = product(
            (high_ref[...], low_ref[...]), (maty[0][columns], maty[1][columns]), NT
        )
        one, two = solved[:rows], solved[rows:]
        out_ref[:, b] = jnp.where(first, one, pltpu.roll(two, half, 1)).reshape(slabs, depth, width)
        out_ref[:, b + 1] = jnp.where(first, pltpu.roll(one, half, 1), two).reshape(
            slabs, depth, width
        )


def plane_solve(planes, inverse_z, inverse_y):
    slabs, blocks, depth, width = planes.shape
    nz, ny = inverse_z.shape[0], inverse_y.shape[0]
    return pl.pallas_call(
        plane_kernel,
        in_specs=[VMEM] * 3,
        out_specs=VMEM,
        out_shape=jax.ShapeDtypeStruct(planes.shape, jnp.float32),
        scratch_shapes=[pltpu.VMEM((2 * nz, ny), jnp.bfloat16)] * 2,
        compiler_params=pltpu.CompilerParams(vmem_limit_bytes=40 * 1024 * 1024),
        cost_estimate=pl.CostEstimate(
            flops=12 * nz * ny * (nz + ny), bytes_accessed=16 * nz * ny, transcendentals=0
        ),
        name="plane_solve",
    )(planes, inverse_z, inverse_y)


def unpack_kernel(in_ref, out_ref):
    sources, depth, width = in_ref.shape
    ny = width // 2
    for z in range(depth):
        turned = in_ref[:, z, :].T
        out_ref[z, :, :sources] = turned[:ny]
        out_ref[z, :, sources:] = turned[ny:]


def unpack(tiles):
    sources, depth, width = tiles.shape
    return pl.pallas_call(
        unpack_kernel,
        in_specs=[VMEM],
        out_specs=VMEM,
        out_shape=jax.ShapeDtypeStruct((depth, width // 2, 2 * sources), jnp.float32),
        cost_estimate=pl.CostEstimate(
            flops=0, bytes_accessed=8 * sources * depth * width, transcendentals=0
        ),
        name="unpack",
    )(tiles)


def edges(values, axis):
    count = lax.axis_size(axis)
    up = [(i, i + 1) for i in range(count - 1)]
    down = [(i + 1, i) for i in range(count - 1)]
    head, tail = values
    return lax.ppermute(tail, axis, up), lax.ppermute(head, axis, down)


def shards(
    potential,
    fast_gate,
    slow_gate,
    tissue,
    region_ids,
    fibre_table,
    inverse_x,
    inverse_z,
    inverse_y,
):
    zlo, zhi = edges((potential[0], potential[-1]), "gz")
    rows_lo = jnp.concatenate([zlo[:1], potential[:, 0], zhi[:1]], axis=0)
    rows_hi = jnp.concatenate([zlo[-1:], potential[:, -1], zhi[-1:]], axis=0)
    ylo, yhi = edges((rows_lo, rows_hi), "gy")
    excited, new_fast, new_slow = ionic(potential, fast_gate, slow_gate, tissue)
    tiles = cross_solve(
        fibre_table, potential, excited, zlo, zhi, ylo, yhi, region_ids[0], inverse_x
    )
    axes = ("gz", "gy")
    planes = lax.all_to_all(tiles, axes, split_axis=0, concat_axis=0, tiled=True)
    slabs, blocks = lax.axis_size("gz"), lax.axis_size("gy")
    solved = plane_solve(planes.reshape((slabs, blocks) + planes.shape[1:]), inverse_z, inverse_y)
    back = lax.all_to_all(
        solved.reshape(planes.shape), axes, split_axis=0, concat_axis=0, tiled=True
    )
    return (unpack(back), new_fast, new_slow)


def solution(mesh):
    return jax.shard_map(
        shards,
        mesh=mesh,
        in_specs=(
            P("gz", "gy", None),
            P("gz", "gy", None),
            P("gz", "gy", None),
            P("gz", "gy", None),
            P("gz", "gy", None),
            P(),
            P(),
            P(),
            P(),
        ),
        out_specs=(P("gz", "gy", None), P("gz", "gy", None), P("gz", "gy", None)),
        check_vma=False,
    )
```

time: 165 us -> 119 us (0.72)
  blocking collectives: 112 us -> 84.6 us
  local copies, waits for them, and re-layouts: 20.5 us -> 3.33 us
  Pallas kernels: 0 us -> 15.3 us
  other arithmetic: 10.8 us -> 0.02 us
  matrix products: 7.7 us -> 0 us
  waiting for transfers between devices: 0.01 us -> 3.05 us
  starting transfers between devices: 12.3 us -> 10.5 us
    all_to_all x4 -> x2, blocking collectives: 112 us -> 84.6 us  [the longest x1 47.2 us: shards(): lax.all_to_all(tiles, axes, split_axis=0, concat_axis=0, tiled=True)]
    mul x7 -> x0, local copies, waits for them, and re-layouts: 15.4 us -> none  [the longest x6 14.6 us: blockwise(): return (shaped * weight[:, None, :, None, :, None]).reshape(field.shape)]
    pallas_call x0 -> x4, Pallas kernels: none -> 15.3 us  [the longest x1 6.77 us: ionic(): pl.pallas_call(ionic_kernel, grid=(nz,), in_specs=[block] * 4, out_specs=...]
    dot_general x3 -> x0, matrix products: 7.7 us -> none  [the longest x1 3.47 us: shards(): jnp.einsum('ij,zjx->zix', inverse_y, y_blocks, precision=lax.Precision.HI...]
    select_n x2 -> x0, other arithmetic: 5.01 us -> none  [the longest x1 3.5 us: ionic(): jnp.where(living, new_slow, slow_gate)]
    add x1 -> x0, other arithmetic: 4.1 us -> none  [shards(): rhs = excited + cross_term(bordered, region_ids, fibre_table)]
    ppermute x4, waiting for transfers between devices: 0.01 us -> 3.05 us  [edges(): return (lax.ppermute(tail, axis, up), lax.ppermute(head, axis, down))]
    ppermute x4, starting transfers between devices: 12.3 us -> 10.5 us  [edges(): return (lax.ppermute(tail, axis, up), lax.ppermute(head, axis, down))]
  transfers between devices with their start and end apart: 4 -> 4, of which waited for: 0 -> 1; matrix products, arithmetic and copies ran while one was open for 12% -> 1% of each run, Pallas kernels for 0% -> 6%
where the time goes in v1:
time: 119 us; the launch traced here: 118 us
  blocking collectives  84.6 us (71%)
  Pallas kernels  15.3 us (13%)
  starting transfers between devices  10.5 us (9%)
  local copies, waits for them, and re-layouts  3.33 us (3%)
  waiting for transfers between devices  3.05 us (3%)
    all_to_all x1, blocking collectives, shards(): lax.all_to_all(tiles, axes, split_axis=0, concat_axis=0, tiled=True)  47.2 us
    all_to_all x1, blocking collectives, shards(): lax.all_to_all(solved.reshape(planes.shape), axes, split_axis=0, concat_a...  37.4 us
    ppermute x4, starting transfers between devices, edges(): return (lax.ppermute(tail, axis, up), lax.ppermute(head, axis, down))  10.5 us
    pallas_call x1, Pallas kernels, ionic(): pl.pallas_call(ionic_kernel, grid=(nz,), in_specs=[block] * 4, out_specs=...  6.77 us
    pallas_call x1, Pallas kernels, cross_solve(): pl.pallas_call(cross_kernel, in_specs=[SMEM] + [VMEM] * 8, out_specs=VMEM...  3.42 us
    ppermute x4, waiting for transfers between devices, edges(): return (lax.ppermute(tail, axis, up), lax.ppermute(head, axis, down))  3.05 us
    pallas_call x1, Pallas kernels, unpack(): pl.pallas_call(unpack_kernel, in_specs=[VMEM], out_specs=VMEM, out_shape=...  2.82 us
  transfers between devices with their start and end apart: 4, of which 1 were waited for; matrix products, arithmetic and copies ran while one was open for 1% of the time, Pallas kernels for 6%

profile of v1, /device:TPU:32, one launch (start us, length us, event | category | flops | bytes accessed | tf_op | source)
XLA Modules:
  0.0 117.6 jit_solution(5591271450526792696)
XLA Ops:
  0.6 1.0 slice_bitcast_fusion
  1.6 1.9 %collective-permute-start.1 = (f32[64,512]{1,0:T(8,128)S(1)}, f32[64,512]{1,0:T(8,128)S(1)}, u32[]{:S(2)}, u32[]{:S(2)}) collective-permute-start(f32[64,512]{1,0:T(8,128)S(1)} %get-tuple-element.11), channel_id=1, source_target_pairs={{8,0},{16,8},{24,16},{32,24},{40,32},{48,40},{56,48},{64,56},{72,6... | collective-permute-start | bytes 393224 | tf_op jit(solution)/shard_map/ppermute | solution.py:249
  3.5 2.4 %collective-permute-start = (f32[64,512]{1,0:T(8,128)S(1)}, f32[64,512]{1,0:T(8,128)S(1)}, u32[]{:S(2)}, u32[]{:S(2)}) collective-permute-start(f32[64,512]{1,0:T(8,128)S(1)} %get-tuple-element.12), channel_id=1, source_target_pairs={{0,8},{8,16},{16,24},{24,32},{32,40},{40,48},{48,56},{56,64},{64,7... | collective-permute-start | bytes 393224 | tf_op jit(solution)/shard_map/ppermute | solution.py:249
  6.0 1.0 fusion
  7.0 0.0 collective-permute-done.1.zhi_ref
  7.0 3.0 %collective-permute-done.zlo_ref = f32[64,512]{1,0:T(8,128)S(1)} collective-permute-done((f32[64,512]{1,0:T(8,128)S(1)}, f32[64,512]{1,0:T(8,128)S(1)}, u32[]{:S(2)}, u32[]{:S(2)}) %collective-permute-start) | collective-permute-done | bytes 131104 | tf_op jit(solution)/shard_map/ppermute | solution.py:249
  10.1 4.9 %collective-permute-start.2 = (f32[10,512]{1,0:T(8,128)S(1)}, f32[10,512]{1,0:T(8,128)S(1)}, u32[]{:S(2)}, u32[]{:S(2)}) collective-permute-start(f32[10,512]{1,0:T(8,128)S(1)} %pad_maximum_fusion), channel_id=1, source_target_pairs={{0,1},{1,2},{2,3},{3,4},{4,5},{5,6},{6,7},{8,9},{9,10},{10,11},{11... | collective-permute-start | bytes 61448 | tf_op jit(solution)/shard_map/ppermute | solution.py:249
  15.0 0.0 copy-start.6
  15.0 1.3 %collective-permute-start.3 = (f32[10,512]{1,0:T(8,128)S(1)}, f32[10,512]{1,0:T(8,128)S(1)}, u32[]{:S(2)}, u32[]{:S(2)}) collective-permute-start(f32[10,512]{1,0:T(8,128)S(1)} %pad_maximum_fusion.1), channel_id=1, source_target_pairs={{1,0},{2,1},{3,2},{4,3},{5,4},{6,5},{7,6},{9,8},{10,9},{11,10},{12... | collective-permute-start | bytes 61448 | tf_op jit(solution)/shard_map/ppermute | solution.py:249
  16.3 0.0 copy-done.6
  16.3 0.1 copy.14.table_ref
  16.4 6.8 %ionic.1 = (f32[8,64,512]{2,1,0:T(8,128)}, f32[8,64,512]{2,1,0:T(8,128)}, f32[8,64,512]{2,1,0:T(8,128)}) custom-call(f32[8,64,512]{2,1,0:T(8,128)} %pot_ref.3, f32[8,64,512]{2,1,0:T(8,128)} %fast_ref.1, f32[8,64,512]{2,1,0:T(8,128)} %slow_ref.1, s32[8,64,512]{2,1,0:T(8,128)} %tissue_ref.1), custom_call_target="tpu_custom_call" | custom-call | flops 10485760 | bytes 7340032 | tf_op jit(solution)/shard_map/ionic/pallas_call | solution.py:75
  23.2 0.0 collective-permute-done.2.ylo_ref
  23.2 0.0 collective-permute-done.3.yhi_ref
  23.2 0.0 copy-done
  23.2 0.0 copy-start.2
  23.2 1.2 %copy-done.2 = f32[8,64,512]{2,1,0:T(8,128)S(1)} copy-done((f32[8,64,512]{2,1,0:T(8,128)S(1)}, f32[8,64,512]{2,1,0:T(8,128)}, u32[]{:S(2)}) %copy-start.2) | copy-done | bytes 1048600
  24.4 3.4 %cross_solve.1 = f32[256,8,128]{2,1,0:T(8,128)S(1)} custom-call(f32[8,3]{1,0:T(8,128)S(1)} %copy.14.table_ref, f32[8,64,512]{2,1,0:T(8,128)S(1)} %copy-done, f32[8,64,512]{2,1,0:T(8,128)S(1)} %copy-done.2, f32[64,512]{1,0:T(8,128)S(1)} %collective-permute-done.zlo_ref, f32[64,512]{1,0:T(8,128)S(1)} %collective-permute-done.1.zhi_ref, ...), custom_call_target="tpu_custom_call" | custom-call | flops 805306368 | bytes 4194304 | tf_op jit(solution)/shard_map/cross_solve/pallas_call | solution.py:153
  27.9 0.0 copy-start.4
  27.9 0.0 copy-start.5
  27.9 47.2 %all_to_all.10 = f32[256,8,128]{2,1,0:T(8,128)S(1)} all-to-all(f32[256,8,128]{2,1,0:T(8,128)S(1)} %cross_solve.1), channel_id=1, replica_groups=mesh['gz'=32,'gy'=8] {'gz','gy'}, dimensions={0} | all-to-all | bytes 2097152 | tf_op jit(solution)/shard_map/all_to_all | solution.py:272
  75.0 2.3 %plane_solve.1 = f32[32,8,8,128]{3,2,1,0:T(8,128)S(1)} custom-call(f32[32,8,8,128]{3,2,1,0:T(8,128)S(1)} %bitcast.13, f32[256,256]{1,0:T(8,128)S(1)} %copy-done.5, f32[512,512]{1,0:T(8,128)S(1)} %copy-done.4), custom_call_target="tpu_custom_call" | custom-call | flops 1207959552 | bytes 2097152 | tf_op jit(solution)/shard_map/plane_solve/pallas_call | solution.py:207
  77.3 37.4 %all_to_all.11.in_ref = f32[256,8,128]{2,1,0:T(8,128)} all-to-all(f32[256,8,128]{2,1,0:T(8,128)S(1)} %bitcast.14), channel_id=1, replica_groups=mesh['gz'=32,'gy'=8] {'gz','gy'}, dimensions={0} | all-to-all | bytes 2097152 | tf_op jit(solution)/shard_map/all_to_all | solution.py:275
  114.8 2.8 %unpack.1 = f32[8,64,512]{2,1,0:T(8,128)} custom-call(f32[256,8,128]{2,1,0:T(8,128)} %all_to_all.11.in_ref), custom_call_target="tpu_custom_call" | custom-call | bytes 2097152 | tf_op jit(solution)/shard_map/unpack/pallas_call | solution.py:232
  (13 shorter events, 0.1 us)
Async XLA Ops:
  1.6 5.4 %collective-permute-start.1 = (f32[64,512]{1,0:T(8,128)S(1)}, f32[64,512]{1,0:T(8,128)S(1)}, u32[]{:S(2)}, u32[]{:S(2)}) collective-permute-start(f32[64,512]{1,0:T(8,128)S(1)} %get-tuple-element.11), channel_id=1, source_target_pairs={{8,0},{16,8},{24,16},{32,24},{40,32},{48,40},{56,48},{64,56},{72,6... | collective-permute-start | bytes 393224 | tf_op jit(solution)/shard_map/ppermute | solution.py:249
  3.5 6.5 %collective-permute-start = (f32[64,512]{1,0:T(8,128)S(1)}, f32[64,512]{1,0:T(8,128)S(1)}, u32[]{:S(2)}, u32[]{:S(2)}) collective-permute-start(f32[64,512]{1,0:T(8,128)S(1)} %get-tuple-element.12), channel_id=1, source_target_pairs={{0,8},{8,16},{16,24},{24,32},{32,40},{40,48},{48,56},{56,64},{64,7... | collective-permute-start | bytes 393224 | tf_op jit(solution)/shard_map/ppermute | solution.py:249
  10.1 13.1 %collective-permute-start.2 = (f32[10,512]{1,0:T(8,128)S(1)}, f32[10,512]{1,0:T(8,128)S(1)}, u32[]{:S(2)}, u32[]{:S(2)}) collective-permute-start(f32[10,512]{1,0:T(8,128)S(1)} %pad_maximum_fusion), channel_id=1, source_target_pairs={{0,1},{1,2},{2,3},{3,4},{4,5},{5,6},{6,7},{8,9},{9,10},{10,11},{11... | collective-permute-start | bytes 61448 | tf_op jit(solution)/shard_map/ppermute | solution.py:249
  15.0 1.3 %copy-start.6 = (f32[8,3]{0,1:T(4,128)S(1)}, f32[8,3]{0,1:T(4,128)}, u32[]{:S(2)}) copy-start(f32[8,3]{0,1:T(4,128)} %param.14) | copy-start | bytes 292
  15.0 8.2 %collective-permute-start.3 = (f32[10,512]{1,0:T(8,128)S(1)}, f32[10,512]{1,0:T(8,128)S(1)}, u32[]{:S(2)}, u32[]{:S(2)}) collective-permute-start(f32[10,512]{1,0:T(8,128)S(1)} %pad_maximum_fusion.1), channel_id=1, source_target_pairs={{1,0},{2,1},{3,2},{4,3},{5,4},{6,5},{7,6},{9,8},{10,9},{11,10},{12... | collective-permute-start | bytes 61448 | tf_op jit(solution)/shard_map/ppermute | solution.py:249
  16.4 6.8 %copy-start = (f32[8,64,512]{2,1,0:T(8,128)S(1)}, f32[8,64,512]{2,1,0:T(8,128)}, u32[]{:S(2)}) copy-start(f32[8,64,512]{2,1,0:T(8,128)} %pot_ref.3) | copy-start | bytes 3145732
  16.4 6.8 %copy-start.1 = (f32[512,512]{1,0:T(8,128)S(1)}, f32[512,512]{1,0:T(8,128)}, u32[]{:S(2)}) copy-start(f32[512,512]{1,0:T(8,128)} %inv_ref.1) | copy-start | bytes 3145732
  16.4 6.8 %copy-start.3 = (s32[1,8,64]{2,1,0:T(8,128)S(1)}, s32[1,8,64]{2,1,0:T(8,128)}, u32[]{:S(2)}) copy-start(s32[1,8,64]{2,1,0:T(8,128)} %param.13) | copy-start | bytes 6148
  23.2 1.2 %copy-start.2 = (f32[8,64,512]{2,1,0:T(8,128)S(1)}, f32[8,64,512]{2,1,0:T(8,128)}, u32[]{:S(2)}) copy-start(f32[8,64,512]{2,1,0:T(8,128)} %get-tuple-element.6.exc_ref) | copy-start | bytes 3145732
  27.9 47.2 %copy-start.4 = (f32[512,512]{1,0:T(8,128)S(1)}, f32[512,512]{1,0:T(8,128)}, u32[]{:S(2)}) copy-start(f32[512,512]{1,0:T(8,128)} %invy_ref.1) | copy-start | bytes 3145732
  27.9 47.2 %copy-start.5 = (f32[256,256]{1,0:T(8,128)S(1)}, f32[256,256]{1,0:T(8,128)}, u32[]{:S(2)}) copy-start(f32[256,256]{1,0:T(8,128)} %invz_ref.1) | copy-start | bytes 786436

commit v2 on v1

--- a/solution.py
+++ b/solution.py
@@ -23,6 +23,7 @@
 inward_slope = 10.0
 
 VMEM = pl.BlockSpec(memory_space=pltpu.VMEM)
+HBM = pl.BlockSpec(memory_space=pltpu.HBM)
 SMEM = pl.BlockSpec(memory_space=pltpu.SMEM)
 NT = (((1,), (1,)), ((), ()))
 NN = (((1,), (0,)), ((), ()))
@@ -46,10 +47,85 @@
     return dot(lh, rh) + (dot(lh, rl) + dot(ll, rh))
 
 
-def ionic_kernel(pot_ref, fast_ref, slow_ref, tissue_ref, exc_ref, nfast_ref, nslow_ref):
-    p, v, w = pot_ref[...], fast_ref[...], slow_ref[...]
-    living = tissue_ref[...] == 1
-    active = p >= gate_crit
+def ionic_kernel(
+    pot_ref, fast_ref, slow_ref, tissue_ref,
+    potc_ref, exc_ref, low_ref, high_ref, nfast_ref, nslow_ref,
+    fast_v, slow_v, tissue_v, nfast_v, nslow_v, in_sems, out_sems,
+):
+    nz, ny, _ = pot_ref.shape
+    pairs = ((pot_ref, potc_ref), (fast_ref, fast_v), (slow_ref, slow_v), (tissue_ref, tissue_v))
+    loads = [
+        [
+            pltpu.make_async_copy(source.at[z], target.at[z], in_sems.at[k, z])
+            for k, (source, target) in enumerate(pairs)
+        ]
+        for z in range(nz)
+    ]
+    stores = [
+        [
+            pltpu.make_async_copy(source.at[z], target.at[z], out_sems.at[k, z])
+            for k, (source, target) in enumerate(((nfast_v, nfast_ref), (nslow_v, nslow_ref)))
+        ]
+        for z in range(nz)
+    ]
+    for group in loads:
+        for copy in group:
+            copy.start()
+    for z in range(nz):
+        for copy in loads[z]:
+            copy.wait()
+        low_ref[z : z + 1] = potc_ref[z, :1]
+        high_ref[z : z + 1] = potc_ref[z, ny - 1 :]
+        for row in range(0, ny, 8):
+            rows = (z, slice(row, row + 8))
+            p, v, w = potc_ref[rows], fast_v[rows], slow_v[rows]
+            living = tissue_v[rows] == 1
+            active = p >= gate_crit
+            exc_ref[rows] = jnp.where(living, excite(p, v, w, active), p)
+            target = jnp.where(active, 0.0, 1.0)
+            keep_fast = jnp.where(
+                active,
+                decay(vclose_tau),
+                jnp.where(p >= vgate_crit, decay(vopen_high), decay(vopen_low)),
+            )
+            keep_slow = jnp.where(active, decay(wclose_tau), decay(wopen_tau))
+            nfast_v[rows] = jnp.where(living, target + (v - target) * keep_fast, v)
+            nslow_v[rows] = jnp.where(living, target + (w - target) * keep_slow, w)
+        for copy in stores[z]:
+            copy.start()
+    for group in stores:
+        for copy in group:
+            copy.wait()
+
+
+def ionic(potential, fast_gate, slow_gate, tissue):
+    nz, ny, nx = potential.shape
+    shape = jax.ShapeDtypeStruct((nz, ny, nx), jnp.float32)
+    line = pltpu.VMEM((nz, nx), jnp.float32)
+    field = pltpu.VMEM((nz, ny, nx), jnp.float32)
+    return pl.pallas_call(
+        ionic_kernel,
+        in_specs=[HBM] * 4,
+        out_specs=[VMEM] * 4 + [HBM] * 2,
+        out_shape=[field, field, line, line, shape, shape],
+        scratch_shapes=[
+            field,
+            field,
+            pltpu.VMEM((nz, ny, nx), jnp.int32),
+            field,
+            field,
+            pltpu.SemaphoreType.DMA((4, nz)),
+            pltpu.SemaphoreType.DMA((2, nz)),
+        ],
+        compiler_params=pltpu.CompilerParams(vmem_limit_bytes=32 * 1024 * 1024),
+        cost_estimate=pl.CostEstimate(
+            flops=40 * nz * ny * nx, bytes_accessed=24 * nz * ny * nx, transcendentals=0
+        ),
+        name="ionic",
+    )(*(pltpu.with_memory_space_constraint(a, pltpu.HBM) for a in (potential, fast_gate, slow_gate, tissue)))
+
+
+def excite(p, v, w, active):
     current = jnp.where(
         active,
         (1.0 / repol_tau) - v * (1.0 - p) * (p - gate_crit) * (1.0 / depol_tau),
@@ -58,31 +134,7 @@
     current = current - w * (1.0 + jnp.tanh(inward_slope * (p - inward_crit))) * (
         1.0 / (2.0 * inward_tau)
     )
-    exc_ref[...] = jnp.where(living, p - time_step * current, p)
-    target = jnp.where(active, 0.0, 1.0)
-    keep_fast = jnp.where(
-        active, decay(vclose_tau), jnp.where(p >= vgate_crit, decay(vopen_high), decay(vopen_low))
-    )
-    keep_slow = jnp.where(active, decay(wclose_tau), decay(wopen_tau))
-    nfast_ref[...] = jnp.where(living, target + (v - target) * keep_fast, v)
-    nslow_ref[...] = jnp.where(living, target + (w - target) * keep_slow, w)
-
-
-def ionic(potential, fast_gate, slow_gate, tissue):
-    nz, ny, nx = potential.shape
-    block = pl.BlockSpec((1, ny, nx), lambda z: (z, 0, 0))
-    shape = jax.ShapeDtypeStruct((nz, ny, nx), jnp.float32)
-    return pl.pallas_call(
-        ionic_kernel,
-        grid=(nz,),
-        in_specs=[block] * 4,
-        out_specs=[block] * 3,
-        out_shape=[shape] * 3,
-        cost_estimate=pl.CostEstimate(
-            flops=40 * nz * ny * nx, bytes_accessed=28 * nz * ny * nx, transcendentals=0
-        ),
-        name="ionic",
-    )(potential, fast_gate, slow_gate, tissue)
+    return p - time_step * current
 
 
 def lane_difference(values):
@@ -93,13 +145,8 @@
     return jnp.where(lane == width - 1, 0.0, ahead) - jnp.where(lane == 0, 0.0, behind)
 
 
-def cross_kernel(
-    table_ref, pot_ref, exc_ref, zlo_ref, zhi_ref, ylo_ref, yhi_ref, region_ref, inv_ref,
-    out_ref, pad_ref, dy_ref, coef_ref, high_ref, low_ref,
-):
-    nz, ny, nx = pot_ref.shape
-    blocks = nx // 8
-    regions = table_ref.shape[0]
+def coefficients(table_ref, region_ref, nx):
+    blocks = region_ref.shape[1]
     spread = (
         lax.broadcasted_iota(jnp.int32, (blocks, nx), 1) // 8
         == lax.broadcasted_iota(jnp.int32, (blocks, nx), 0)
@@ -108,38 +155,100 @@
         region_ref[...].astype(jnp.float32).astype(jnp.bfloat16), spread, NN,
         preferred_element_type=jnp.float32,
     )
+    coefs = []
     for column in range(3):
         coef = jnp.zeros_like(ids)
-        for region in range(regions):
+        for region in range(table_ref.shape[0]):
             coef = jnp.where(ids == float(region), 0.5 * table_ref[region, column], coef)
+        coefs.append(coef)
+    return coefs
+
+
+def ordered(odd, inner, outer):
+    return jnp.where(odd == 1, inner, outer), jnp.where(odd == 1, outer, inner)
+
+
+def stencil_kernel(
+    table_ref, pot_ref, exc_ref, inner_ref, outer_ref, region_ref, inv_ref,
+    rhs_ref, coef_ref, ihigh_ref, ilow_ref, pad_ref, dy_ref,
+):
+    nz, ny, nx = pot_ref.shape
+    for column, coef in enumerate(coefficients(table_ref, region_ref, nx)):
         coef_ref[column] = coef
-
+    below, above = ordered(lax.axis_index("gz") % 2, inner_ref[...], outer_ref[...])
+    nothing = jnp.zeros((1, nx), jnp.float32)
     for z in range(nz + 2):
-        plane = zlo_ref[...] if z == 0 else zhi_ref[...] if z == nz + 1 else pot_ref[z - 1]
+        plane = below if z == 0 else above if z == nz + 1 else pot_ref[z - 1]
         pad_ref[z, 8 : 8 + ny] = plane
-        pad_ref[z, 7:8] = ylo_ref[z : z + 1]
-        pad_ref[z, 8 + ny : 9 + ny] = yhi_ref[z : z + 1]
+        pad_ref[z, 7:8] = nothing
+        pad_ref[z, 8 + ny : 9 + ny] = nothing
         dy_ref[z] = pad_ref[z, 9 : 9 + ny] - pad_ref[z, 7 : 7 + ny]
-
     for z in range(nz):
-        mixed_xy = lane_difference(dy_ref[z + 1])
-        mixed_xz = lane_difference(pad_ref[z + 2, 8 : 8 + ny] - pad_ref[z, 8 : 8 + ny])
-        mixed_yz = dy_ref[z + 2] - dy_ref[z]
         for b in range(ny // 8):
             rows = slice(8 * b, 8 * b + 8)
-            rhs = exc_ref[z, rows] + (
-                coef_ref[0, b : b + 1] * mixed_xy[rows]
-                + coef_ref[1, b : b + 1] * mixed_xz[rows]
-                + coef_ref[2, b : b + 1] * mixed_yz[rows]
+            inside = slice(8 * b + 8, 8 * b + 16)
+            mixed_xy = lane_difference(dy_ref[z + 1, rows])
+            mixed_xz = lane_difference(pad_ref[z + 2, inside] - pad_ref[z, inside])
+            mixed_yz = dy_ref[z + 2, rows] - dy_ref[z, rows]
+            rhs_ref[z, rows] = exc_ref[z, rows] + (
+                coef_ref[0, b : b + 1] * mixed_xy
+                + coef_ref[1, b : b + 1] * mixed_xz
+                + coef_ref[2, b : b + 1] * mixed_yz
             )
-            pad_ref[0, rows] = rhs
-        high, low = split(pad_ref[0, 0:ny])
-        high_ref[z * ny : (z + 1) * ny] = high
-        low_ref[z * ny : (z + 1) * ny] = low
-
+    ihigh_ref[...], ilow_ref[...] = split(inv_ref[...])
+
+
+def stencil(table, potential, excited, inner, outer, region, inverse_x):
+    nz, ny, nx = potential.shape
+    half = pltpu.VMEM((nx, nx), jnp.bfloat16)
+    return pl.pallas_call(
+        stencil_kernel,
+        in_specs=[SMEM] + [VMEM] * 6,
+        out_specs=[VMEM] * 4,
+        out_shape=[
+            pltpu.VMEM((nz, ny, nx), jnp.float32),
+            pltpu.VMEM((3, ny // 8, nx), jnp.float32),
+            half,
+            half,
+        ],
+        scratch_shapes=[
+            pltpu.VMEM((nz + 2, ny + 16, nx), jnp.float32),
+            pltpu.VMEM((nz + 2, ny, nx), jnp.float32),
+        ],
+        compiler_params=pltpu.CompilerParams(vmem_limit_bytes=32 * 1024 * 1024),
+        cost_estimate=pl.CostEstimate(
+            flops=60 * nz * ny * nx, bytes_accessed=20 * nz * ny * nx, transcendentals=0
+        ),
+        name="stencil",
+    )(table, potential, excited, inner, outer, region, inverse_x)
+
+
+def line_kernel(
+    rhs_ref, inner_ref, outer_ref, coef_ref, ihigh_ref, ilow_ref,
+    out_ref, edge_ref, high_ref, low_ref,
+):
+    nz, ny, nx = rhs_ref.shape
     half = nx // 2
-    matrix = split(inv_ref[...])
+    matrix = ihigh_ref[...], ilow_ref[...]
+    sides = ordered(lax.axis_index("gy") % 2, inner_ref[...], outer_ref[...])
+    for side, block, sign in ((0, 0, -1.0), (1, ny // 8 - 1, 1.0)):
+        line = sides[side]
+        row = slice(block, block + 1)
+        mixed = coef_ref[0, row] * lane_difference(line)[1 : nz + 1] + coef_ref[2, row] * (
+            line[2 : nz + 2] - line[:nz]
+        )
+        edge_ref[side] = sign * mixed
+    row = lax.broadcasted_iota(jnp.int32, (8, nx), 0)
     first = lax.broadcasted_iota(jnp.int32, (half, 2 * ny), 1) < ny
+    for z in range(nz):
+        for b in range(ny // 8):
+            part = rhs_ref[z, 8 * b : 8 * b + 8]
+            if b == 0:
+                part = part + jnp.where(row == 0, edge_ref[0, z : z + 1], 0.0)
+            if b == ny // 8 - 1:
+                part = part + jnp.where(row == 7, edge_ref[1, z : z + 1], 0.0)
+            rows = slice(z * ny + 8 * b, z * ny + 8 * b + 8)
+            high_ref[rows], low_ref[rows] = split(part)
     for z in range(0, nz, 2):
         rows = slice(z * ny, (z + 2) * ny)
         solved = product(matrix, (high_ref[rows], low_ref[rows]), NT)
@@ -148,26 +257,24 @@
         out_ref[:, z + 1, :] = jnp.where(first, pltpu.roll(lower, ny, 1), upper)
 
 
-def cross_solve(table, potential, excited, zlo, zhi, ylo, yhi, region, inverse_x):
-    nz, ny, nx = potential.shape
+def line_solve(rhs, inner, outer, coefs, inv_high, inv_low):
+    nz, ny, nx = rhs.shape
     return pl.pallas_call(
-        cross_kernel,
-        in_specs=[SMEM] + [VMEM] * 8,
+        line_kernel,
+        in_specs=[VMEM] * 6,
         out_specs=VMEM,
         out_shape=jax.ShapeDtypeStruct((nx // 2, nz, 2 * ny), jnp.float32),
         scratch_shapes=[
-            pltpu.VMEM((nz + 2, ny + 16, nx), jnp.float32),
-            pltpu.VMEM((nz + 2, ny, nx), jnp.float32),
-            pltpu.VMEM((3, ny // 8, nx), jnp.float32),
+            pltpu.VMEM((2, nz, nx), jnp.float32),
             pltpu.VMEM((nz * ny, nx), jnp.bfloat16),
             pltpu.VMEM((nz * ny, nx), jnp.bfloat16),
         ],
-        compiler_params=pltpu.CompilerParams(vmem_limit_bytes=40 * 1024 * 1024),
+        compiler_params=pltpu.CompilerParams(vmem_limit_bytes=32 * 1024 * 1024),
         cost_estimate=pl.CostEstimate(
-            flops=6 * nz * ny * nx * nx, bytes_accessed=16 * nz * ny * nx, transcendentals=0
-        ),
-        name="cross_solve",
-    )(table, potential, excited, zlo, zhi, ylo, yhi, region, inverse_x)
+            flops=6 * nz * ny * nx * nx, bytes_accessed=12 * nz * ny * nx, transcendentals=0
+        ),
+        name="line_solve",
+    )(rhs, inner, outer, coefs, inv_high, inv_low)
 
 
 def plane_kernel(in_ref, invz_ref, invy_ref, out_ref, high_ref, low_ref):
@@ -241,12 +348,14 @@
     )(tiles)
 
 
-def edges(values, axis):
+def swaps(axis, inner, outer):
     count = lax.axis_size(axis)
-    up = [(i, i + 1) for i in range(count - 1)]
-    down = [(i + 1, i) for i in range(count - 1)]
-    head, tail = values
-    return lax.ppermute(tail, axis, up), lax.ppermute(head, axis, down)
+
+    def both(first):
+        pairs = [(i, i + 1) for i in range(first, count - 1, 2)]
+        return pairs + [(j, i) for i, j in pairs]
+
+    return lax.ppermute(outer, axis, both(1)), lax.ppermute(inner, axis, both(0))
 
 
 def shards(
@@ -260,14 +369,29 @@
     inverse_z,
     inverse_y,
 ):
-    zlo, zhi = edges((potential[0], potential[-1]), "gz")
-    rows_lo = jnp.concatenate([zlo[:1], potential[:, 0], zhi[:1]], axis=0)
-    rows_hi = jnp.concatenate([zlo[-1:], potential[:, -1], zhi[-1:]], axis=0)
-    ylo, yhi = edges((rows_lo, rows_hi), "gy")
-    excited, new_fast, new_slow = ionic(potential, fast_gate, slow_gate, tissue)
-    tiles = cross_solve(
-        fibre_table, potential, excited, zlo, zhi, ylo, yhi, region_ids[0], inverse_x
-    )
+    odd = lax.axis_index("gz") % 2
+    first, last = potential[0], potential[-1]
+    z_outer, z_inner = swaps(
+        "gz", jnp.where(odd == 1, first, last), jnp.where(odd == 1, last, first)
+    )
+    held, excited, row_low, row_high, new_fast, new_slow = ionic(
+        potential, fast_gate, slow_gate, tissue
+    )
+    z_outer, z_inner, row_low, row_high = lax.optimization_barrier(
+        (z_outer, z_inner, row_low, row_high)
+    )
+    last = z_inner.shape[0] - 1
+    below, above = ordered(odd, z_inner[::last], z_outer[::last])
+    row_low = jnp.concatenate([below[:1], row_low, above[:1]], axis=0)
+    row_high = jnp.concatenate([below[1:], row_high, above[1:]], axis=0)
+    odd = lax.axis_index("gy") % 2
+    y_outer, y_inner = swaps(
+        "gy", jnp.where(odd == 1, row_low, row_high), jnp.where(odd == 1, row_high, row_low)
+    )
+    rhs, coefs, inv_high, inv_low = stencil(
+        fibre_table, held, excited, z_inner, z_outer, region_ids[0], inverse_x
+    )
+    tiles = line_solve(rhs, y_inner, y_outer, coefs, inv_high, inv_low)
     axes = ("gz", "gy")
     planes = lax.all_to_all(tiles, axes, split_axis=0, concat_axis=0, tiled=True)
     slabs, blocks = lax.axis_size("gz"), lax.axis_size("gy")

time: 119 us -> 111 us (0.933)
  waiting for transfers between devices: 3.05 us -> 0.01 us
  starting transfers between devices: 10.5 us -> 7.95 us
  local copies, waits for them, and re-layouts: 3.33 us -> 0.84 us
  Pallas kernels: 15.3 us -> 13.1 us
  other arithmetic: 0.02 us -> 1.72 us
    ppermute x4, waiting for transfers between devices: 3.05 us -> 0.01 us  [the longest x2 0.01 us: swaps(): lax.ppermute(inner, axis, both(0))]
    ppermute x4, starting transfers between devices: 10.5 us -> 7.95 us  [the longest x2 5.39 us: swaps(): lax.ppermute(inner, axis, both(0))]
    pallas_call x2 -> x3, Pallas kernels: 10.2 us -> 7.97 us  [the longest x1 3.69 us: ionic(): pl.pallas_call(ionic_kernel, in_specs=[HBM] * 4, out_specs=[VMEM] * 4 + [...]
    select_n x0 -> x3, other arithmetic: none -> 1.72 us  [the longest x1 1.69 us: shards(): jnp.where(odd == 1, first, last)]
  transfers between devices with their start and end apart: 4 -> 4, of which waited for: 1 -> 0; matrix products, arithmetic and copies ran while one was open for 1% -> 0% of each run, Pallas kernels for 6% -> 5%
where the time goes in v2:
time: 111 us; the launch traced here: 109 us
  blocking collectives  84.9 us (76%)
  Pallas kernels  13.1 us (12%)
  starting transfers between devices  7.95 us (7%)
  other arithmetic  1.72 us (2%)
    all_to_all x1, blocking collectives, shards(): lax.all_to_all(tiles, axes, split_axis=0, concat_axis=0, tiled=True)  47.5 us
    all_to_all x1, blocking collectives, shards(): lax.all_to_all(solved.reshape(planes.shape), axes, split_axis=0, concat_a...  37.4 us
    ppermute x2, starting transfers between devices, swaps(): lax.ppermute(inner, axis, both(0))  5.39 us
    pallas_call x1, Pallas kernels, ionic(): pl.pallas_call(ionic_kernel, in_specs=[HBM] * 4, out_specs=[VMEM] * 4 + [...  3.69 us
    pallas_call x1, Pallas kernels, unpack(): pl.pallas_call(unpack_kernel, in_specs=[VMEM], out_specs=VMEM, out_shape=...  2.82 us
    ppermute x2, starting transfers between devices, swaps(): lax.ppermute(outer, axis, both(1))  2.56 us
    pallas_call x1, Pallas kernels, plane_solve(): pl.pallas_call(plane_kernel, in_specs=[VMEM] * 3, out_specs=VMEM, out_sha...  2.29 us
    pallas_call x1, Pallas kernels, line_solve(): pl.pallas_call(line_kernel, in_specs=[VMEM] * 6, out_specs=VMEM, out_shap...  2.25 us
  transfers between devices with their start and end apart: 4, of which 0 were waited for; matrix products, arithmetic and copies ran while one was open for 0% of the time, Pallas kernels for 5%

profile of v2, /device:TPU:32, one launch (start us, length us, event | category | flops | bytes accessed | tf_op | source)
XLA Modules:
  0.0 109.3 jit_solution(9580347058814507645)
XLA Ops:
  0.6 1.7 %select_bitcast_fusion = (f32[64,512]{1,0:T(8,128)}, f32[64,512]{1,0:T(8,128)}) fusion(f32[8,64,512]{2,1,0:T(8,128)} %pot_ref.1, pred[]{:T(512)S(6)} %eq.7), kind=kLoop, calls=%fused_computation | loop fusion | flops 65536 | bytes 524289 | tf_op jit(solution)/shard_map/jit(_where)/select_n | solution.py:375
  2.3 1.9 %collective-permute-start = (f32[64,512]{1,0:T(8,128)}, f32[64,512]{1,0:T(8,128)S(1)}, u32[]{:S(2)}, u32[]{:S(2)}) collective-permute-start(f32[64,512]{1,0:T(8,128)} %get-tuple-element.32), channel_id=1, source_target_pairs={{8,16},{24,32},{40,48},{56,64},{72,80},{88,96},{104,112},{120,128}... | collective-permute-start | bytes 393224 | tf_op jit(solution)/shard_map/ppermute | solution.py:358
  4.2 2.1 %collective-permute-start.1 = (f32[64,512]{1,0:T(8,128)}, f32[64,512]{1,0:T(8,128)S(1)}, u32[]{:S(2)}, u32[]{:S(2)}) collective-permute-start(f32[64,512]{1,0:T(8,128)} %get-tuple-element.31), channel_id=1, source_target_pairs={{0,8},{16,24},{32,40},{48,56},{64,72},{80,88},{96,104},{112,120},{... | collective-permute-start | bytes 393224 | tf_op jit(solution)/shard_map/ppermute | solution.py:358
  6.4 3.7 %ionic.1 = (f32[8,64,512]{2,1,0:T(8,128)S(1)}, f32[8,64,512]{2,1,0:T(8,128)S(1)}, f32[8,512]{1,0:T(8,128)S(1)}, f32[8,512]{1,0:T(8,128)S(1)}, f32[8,64,512]{2,1,0:T(8,128)}, /*index=5*/f32[8,64,512]{2,1,0:T(8,128)}) custom-call(f32[8,64,512]{2,1,0:T(8,128)} %pot_ref.1, f32[8,64,512]{2,1,0:T(8,128)} %fast_ref.1, f32[8,64,512]{2,1,0:T(8,128)} %slow_ref.1, ...), custom_call_target="tpu_custom_call" | custom-call | flops 10485760 | bytes 6291456 | tf_op jit(solution)/shard_map/ionic/pallas_call | solution.py:106
  10.1 0.0 collective-permute-done.outer_ref
  10.1 0.0 collective-permute-done.1.inner_ref
  10.2 0.0 copy-start.4
  10.2 3.3 %collective-permute-start.2 = (f32[10,512]{1,0:T(8,128)S(1)}, f32[10,512]{1,0:T(8,128)S(1)}, u32[]{:S(2)}, u32[]{:S(2)}) collective-permute-start(f32[10,512]{1,0:T(8,128)S(1)} %get-tuple-element.34), channel_id=1, source_target_pairs={{0,1},{2,3},{4,5},{6,7},{1,0},{3,2},{5,4},{7,6},{8,9},{10,11},{12,... | collective-permute-start | bytes 61448 | tf_op jit(solution)/shard_map/ppermute | solution.py:358
  13.5 0.7 collective-permute-start.3
  14.1 0.0 copy-done.4
  14.1 0.1 copy.12.table_ref
  14.2 0.0 copy-done
  14.2 0.7 copy-done.1
  14.9 2.0 %stencil.1 = (f32[8,64,512]{2,1,0:T(8,128)S(1)}, f32[3,8,512]{2,1,0:T(8,128)S(1)}, bf16[512,512]{1,0:T(8,128)(2,1)S(1)}, bf16[512,512]{1,0:T(8,128)(2,1)S(1)}) custom-call(f32[8,3]{1,0:T(8,128)S(1)} %copy.12.table_ref, f32[8,64,512]{2,1,0:T(8,128)S(1)} %get-tuple-element.17.pot_ref, f32[8,64,512]{2,1,0:T(8,128)S(1)} %get-tuple-element.18.exc_ref, ...), custom_call_target="tpu_custom_call" | custom-call | flops 15728640 | bytes 5242880 | tf_op jit(solution)/shard_map/stencil/pallas_call | solution.py:204
  16.9 0.0 collective-permute-done.2.inner_ref
  16.9 0.0 collective-permute-done.3.outer_ref
  17.0 2.2 %line_solve.1 = f32[256,8,128]{2,1,0:T(8,128)S(1)} custom-call(f32[8,64,512]{2,1,0:T(8,128)S(1)} %get-tuple-element.23.rhs_ref, f32[10,512]{1,0:T(8,128)S(1)} %collective-permute-done.2.inner_ref, f32[10,512]{1,0:T(8,128)S(1)} %collective-permute-done.3.outer_ref, f32[3,8,512]{2,1,0:T(8,128)S(1)} %get-tuple-element.26.coef_ref, ...), custom_call_target="tpu_custom_call" | custom-call | flops 805306368 | bytes 3145728 | tf_op jit(solution)/shard_map/line_solve/pallas_call | solution.py:262
  19.2 0.0 copy-start.2
  19.2 0.0 copy-start.3
  19.2 47.5 %all_to_all.10 = f32[256,8,128]{2,1,0:T(8,128)S(1)} all-to-all(f32[256,8,128]{2,1,0:T(8,128)S(1)} %line_solve.1), channel_id=1, replica_groups=mesh['gz'=32,'gy'=8] {'gz','gy'}, dimensions={0} | all-to-all | bytes 2097152 | tf_op jit(solution)/shard_map/all_to_all | solution.py:396
  66.7 0.0 copy-done.2
  66.7 2.3 %plane_solve.1 = f32[32,8,8,128]{3,2,1,0:T(8,128)S(1)} custom-call(f32[32,8,8,128]{3,2,1,0:T(8,128)S(1)} %bitcast.7, f32[256,256]{1,0:T(8,128)S(1)} %copy-done.3, f32[512,512]{1,0:T(8,128)S(1)} %copy-done.2), custom_call_target="tpu_custom_call" | custom-call | flops 1207959552 | bytes 2097152 | tf_op jit(solution)/shard_map/plane_solve/pallas_call | solution.py:314
  69.0 37.4 %all_to_all.11.in_ref = f32[256,8,128]{2,1,0:T(8,128)} all-to-all(f32[256,8,128]{2,1,0:T(8,128)S(1)} %bitcast.8), channel_id=1, replica_groups=mesh['gz'=32,'gy'=8] {'gz','gy'}, dimensions={0} | all-to-all | bytes 2097152 | tf_op jit(solution)/shard_map/all_to_all | solution.py:399
  106.5 2.8 %unpack.1 = f32[8,64,512]{2,1,0:T(8,128)} custom-call(f32[256,8,128]{2,1,0:T(8,128)} %all_to_all.11.in_ref), custom_call_target="tpu_custom_call" | custom-call | bytes 2097152 | tf_op jit(solution)/shard_map/unpack/pallas_call | solution.py:339
  (8 shorter events, 0.1 us)
Async XLA Ops:
  2.3 7.7 %collective-permute-start = (f32[64,512]{1,0:T(8,128)}, f32[64,512]{1,0:T(8,128)S(1)}, u32[]{:S(2)}, u32[]{:S(2)}) collective-permute-start(f32[64,512]{1,0:T(8,128)} %get-tuple-element.32), channel_id=1, source_target_pairs={{8,16},{24,32},{40,48},{56,64},{72,80},{88,96},{104,112},{120,128}... | collective-permute-start | bytes 393224 | tf_op jit(solution)/shard_map/ppermute | solution.py:358
  4.2 5.8 %collective-permute-start.1 = (f32[64,512]{1,0:T(8,128)}, f32[64,512]{1,0:T(8,128)S(1)}, u32[]{:S(2)}, u32[]{:S(2)}) collective-permute-start(f32[64,512]{1,0:T(8,128)} %get-tuple-element.31), channel_id=1, source_target_pairs={{0,8},{16,24},{32,40},{48,56},{64,72},{80,88},{96,104},{112,120},{... | collective-permute-start | bytes 393224 | tf_op jit(solution)/shard_map/ppermute | solution.py:358
  6.4 7.9 %copy-start = (f32[512,512]{1,0:T(8,128)S(1)}, f32[512,512]{1,0:T(8,128)}, u32[]{:S(2)}) copy-start(f32[512,512]{1,0:T(8,128)} %inv_ref.1) | copy-start | bytes 3145732
  10.2 4.0 %copy-start.4 = (f32[8,3]{0,1:T(4,128)S(1)}, f32[8,3]{0,1:T(4,128)}, u32[]{:S(2)}) copy-start(f32[8,3]{0,1:T(4,128)} %param.14) | copy-start | bytes 292
  10.2 6.8 %collective-permute-start.2 = (f32[10,512]{1,0:T(8,128)S(1)}, f32[10,512]{1,0:T(8,128)S(1)}, u32[]{:S(2)}, u32[]{:S(2)}) collective-permute-start(f32[10,512]{1,0:T(8,128)S(1)} %get-tuple-element.34), channel_id=1, source_target_pairs={{0,1},{2,3},{4,5},{6,7},{1,0},{3,2},{5,4},{7,6},{8,9},{10,11},{12,... | collective-permute-start | bytes 61448 | tf_op jit(solution)/shard_map/ppermute | solution.py:358
  13.5 3.5 %collective-permute-start.3 = (f32[10,512]{1,0:T(8,128)S(1)}, f32[10,512]{1,0:T(8,128)S(1)}, u32[]{:S(2)}, u32[]{:S(2)}) collective-permute-start(f32[10,512]{1,0:T(8,128)S(1)} %get-tuple-element.33), channel_id=1, source_target_pairs={{1,2},{3,4},{5,6},{2,1},{4,3},{6,5},{9,10},{11,12},{13,14},{10,9},... | collective-permute-start | bytes 61448 | tf_op jit(solution)/shard_map/ppermute | solution.py:358
  14.2 0.7 copy-start.1
  19.2 47.5 %copy-start.2 = (f32[512,512]{1,0:T(8,128)S(1)}, f32[512,512]{1,0:T(8,128)}, u32[]{:S(2)}) copy-start(f32[512,512]{1,0:T(8,128)} %invy_ref.1) | copy-start | bytes 3145732
  19.2 47.5 %copy-start.3 = (f32[256,256]{1,0:T(8,128)S(1)}, f32[256,256]{1,0:T(8,128)}, u32[]{:S(2)}) copy-start(f32[256,256]{1,0:T(8,128)} %invz_ref.1) | copy-start | bytes 786436

commit v3 on v2

v3 whole, which is shorter than its diff:
```python
import math

import jax
import jax.numpy as jnp
from jax import lax
from jax.experimental import pallas as pl
from jax.experimental.pallas import tpu as pltpu
from jax.sharding import PartitionSpec as P

time_step = 0.1
depol_tau = 0.25
repol_tau = 33.33
inward_tau = 29.0
outward_tau = 12.5
vclose_tau = 3.33
vopen_high = 19.6
vopen_low = 1250.0
wclose_tau = 870.0
wopen_tau = 41.0
gate_crit = 0.13
vgate_crit = 0.04
inward_crit = 0.85
inward_slope = 10.0

VMEM = pl.BlockSpec(memory_space=pltpu.VMEM)
HBM = pl.BlockSpec(memory_space=pltpu.HBM)
NT = (((1,), (1,)), ((), ()))
NN = (((1,), (0,)), ((), ()))


def decay(tau):
    return math.exp(-time_step / tau)


def split(values):
    high = values.astype(jnp.bfloat16)
    return high, (values - high.astype(jnp.float32)).astype(jnp.bfloat16)


def product(left, right, dims):
    (lh, ll), (rh, rl) = left, right

    def dot(a, b):
        return lax.dot_general(a, b, dims, preferred_element_type=jnp.float32)

    return dot(lh, rh) + (dot(lh, rl) + dot(ll, rh))


def pinned(*arrays):
    return [pltpu.with_memory_space_constraint(array, pltpu.HBM) for array in arrays]


def faces_kernel(pot_ref, inner_ref, outer_ref, sems):
    odd = lax.axis_index("gz") % 2
    last = pot_ref.shape[0] - 1
    copies = [
        pltpu.make_async_copy(pot_ref.at[last * (1 - odd)], inner_ref, sems.at[0]),
        pltpu.make_async_copy(pot_ref.at[last * odd], outer_ref, sems.at[1]),
    ]
    for copy in copies:
        copy.start()
    for copy in copies:
        copy.wait()


def faces(potential):
    plane = pltpu.VMEM(potential.shape[1:], jnp.float32)
    return pl.pallas_call(
        faces_kernel,
        in_specs=[HBM],
        out_specs=[VMEM] * 2,
        out_shape=[plane] * 2,
        scratch_shapes=[pltpu.SemaphoreType.DMA((2,))],
        name="faces",
    )(*pinned(potential))


def ionic_kernel(
    table_ref, pot_ref, fast_ref, slow_ref, tissue_ref, region_ref, inv_ref,
    potc_ref, exc_ref, rows_ref, coef_ref, ihigh_ref, ilow_ref, nfast_ref, nslow_ref,
    fast_v, slow_v, tissue_v, region_v, inv_v, nfast_v, nslow_v, table_s,
    in_sems, out_sems, sems,
):
    nz, ny, nx = pot_ref.shape
    extra = [
        pltpu.make_async_copy(region_ref, region_v, sems.at[0]),
        pltpu.make_async_copy(inv_ref, inv_v, sems.at[1]),
        pltpu.make_async_copy(table_ref, table_s, sems.at[2]),
    ]
    pairs = ((pot_ref, potc_ref), (fast_ref, fast_v), (slow_ref, slow_v), (tissue_ref, tissue_v))
    loads = [
        [
            pltpu.make_async_copy(source.at[z], target.at[z], in_sems.at[k, z])
            for k, (source, target) in enumerate(pairs)
        ]
        for z in range(nz)
    ]
    stores = [
        [
            pltpu.make_async_copy(source.at[z], target.at[z], out_sems.at[k, z])
            for k, (source, target) in enumerate(((nfast_v, nfast_ref), (nslow_v, nslow_ref)))
        ]
        for z in range(nz)
    ]
    for group in loads:
        for copy in group:
            copy.start()
    for copy in extra:
        copy.start()
    for z in range(nz):
        for copy in loads[z]:
            copy.wait()
        for row in range(0, ny, 8):
            rows = (z, slice(row, row + 8))
            p, v, w = potc_ref[rows], fast_v[rows], slow_v[rows]
            living = tissue_v[rows] == 1
            active = p >= gate_crit
            exc_ref[rows] = jnp.where(living, excite(p, v, w, active), p)
            target = jnp.where(active, 0.0, 1.0)
            keep_fast = jnp.where(
                active,
                decay(vclose_tau),
                jnp.where(p >= vgate_crit, decay(vopen_high), decay(vopen_low)),
            )
            keep_slow = jnp.where(active, decay(wclose_tau), decay(wopen_tau))
            nfast_v[rows] = jnp.where(living, target + (v - target) * keep_fast, v)
            nslow_v[rows] = jnp.where(living, target + (w - target) * keep_slow, w)
        for copy in stores[z]:
            copy.start()
        for k, line in enumerate((potc_ref[z, 0:1], potc_ref[z, 1:2], exc_ref[z, 0:1])):
            rows_ref[k * nz + z : k * nz + z + 1] = line
    for copy in extra:
        copy.wait()
    for column, coef in enumerate(coefficients(table_s, region_v, nx)):
        coef_ref[column] = coef
    ihigh_ref[...], ilow_ref[...] = split(inv_v[...])
    for group in stores:
        for copy in group:
            copy.wait()


def ionic(table, potential, fast_gate, slow_gate, tissue, region, inverse_x):
    nz, ny, nx = potential.shape
    shape = jax.ShapeDtypeStruct((nz, ny, nx), jnp.float32)
    field = pltpu.VMEM((nz, ny, nx), jnp.float32)
    part = pltpu.VMEM((nx, nx), jnp.bfloat16)
    return pl.pallas_call(
        ionic_kernel,
        in_specs=[HBM] * 7,
        out_specs=[VMEM] * 6 + [HBM] * 2,
        out_shape=[
            field,
            field,
            pltpu.VMEM((3 * nz, nx), jnp.float32),
            pltpu.VMEM((3, ny // 8, nx), jnp.float32),
            part,
            part,
            shape,
            shape,
        ],
        scratch_shapes=[
            field,
            field,
            pltpu.VMEM((nz, ny, nx), jnp.int32),
            pltpu.VMEM(region.shape, jnp.int32),
            pltpu.VMEM((nx, nx), jnp.float32),
            field,
            field,
            pltpu.SMEM(table.shape, jnp.float32),
            pltpu.SemaphoreType.DMA((4, nz)),
            pltpu.SemaphoreType.DMA((2, nz)),
            pltpu.SemaphoreType.DMA((3,)),
        ],
        compiler_params=pltpu.CompilerParams(vmem_limit_bytes=16 * 1024 * 1024),
        cost_estimate=pl.CostEstimate(
            flops=40 * nz * ny * nx, bytes_accessed=28 * nz * ny * nx, transcendentals=0
        ),
        name="ionic",
    )(*pinned(table, potential, fast_gate, slow_gate, tissue, region, inverse_x))


def excite(p, v, w, active):
    current = jnp.where(
        active,
        (1.0 / repol_tau) - v * (1.0 - p) * (p - gate_crit) * (1.0 / depol_tau),
        p * (1.0 / outward_tau),
    )
    current = current - w * (1.0 + jnp.tanh(inward_slope * (p - inward_crit))) * (
        1.0 / (2.0 * inward_tau)
    )
    return p - time_step * current


def lane_difference(values):
    width = values.shape[-1]
    lane = lax.broadcasted_iota(jnp.int32, values.shape, values.ndim - 1)
    ahead = pltpu.roll(values, width - 1, values.ndim - 1)
    behind = pltpu.roll(values, 1, values.ndim - 1)
    return jnp.where(lane == width - 1, 0.0, ahead) - jnp.where(lane == 0, 0.0, behind)


def coefficients(table_ref, region_ref, nx):
    blocks = region_ref.shape[1]
    spread = (
        lax.broadcasted_iota(jnp.int32, (blocks, nx), 1) // 8
        == lax.broadcasted_iota(jnp.int32, (blocks, nx), 0)
    ).astype(jnp.bfloat16)
    ids = lax.dot_general(
        region_ref[...].astype(jnp.float32).astype(jnp.bfloat16), spread, NN,
        preferred_element_type=jnp.float32,
    )
    coefs = []
    for column in range(3):
        coef = jnp.zeros_like(ids)
        for region in range(table_ref.shape[1]):
            coef = jnp.where(ids == float(region), 0.5 * table_ref[column, region], coef)
        coefs.append(coef)
    return coefs


def ordered(odd, inner, outer):
    return jnp.where(odd == 1, inner, outer), jnp.where(odd == 1, outer, inner)


def message_kernel(rows_ref, coef_ref, inner_ref, outer_ref, out_ref, pad_ref):
    nz = rows_ref.shape[0] // 3
    pads = nz + 2
    odd = lax.axis_index("gz") % 2
    for k in range(2):
        row = slice(k, k + 1)
        below, above = ordered(odd, inner_ref[row], outer_ref[row])
        pad_ref[k, 0:1] = below
        pad_ref[k, 1 : nz + 1] = rows_ref[k * nz : (k + 1) * nz]
        pad_ref[k, nz + 1 : pads] = above
    out_ref[0:nz] = rows_ref[2 * nz :] + (
        coef_ref[0, 0:1] * lane_difference(pad_ref[1, 1 : nz + 1])
        + coef_ref[1, 0:1] * lane_difference(pad_ref[0, 2:pads] - pad_ref[0, 0:nz])
        + coef_ref[2, 0:1] * (pad_ref[1, 2:pads] - pad_ref[1, 0:nz])
    )
    out_ref[nz : nz + pads] = pad_ref[0, 0:pads]
    out_ref[nz + pads : nz + pads + 1] = coef_ref[0, 0:1]
    out_ref[nz + pads + 1 : nz + pads + 2] = coef_ref[2, 0:1]
    rest = out_ref.shape[0] - (nz + pads + 2)
    out_ref[nz + pads + 2 :] = jnp.zeros((rest, out_ref.shape[1]), jnp.float32)


def message(rows, coefs, inner, outer):
    nz, nx = rows.shape[0] // 3, rows.shape[1]
    return pl.pallas_call(
        message_kernel,
        in_specs=[VMEM] * 4,
        out_specs=VMEM,
        out_shape=pltpu.VMEM((3 * nz, nx), jnp.float32),
        scratch_shapes=[pltpu.VMEM((2, 16, nx), jnp.float32)],
        compiler_params=pltpu.CompilerParams(vmem_limit_bytes=4 * 1024 * 1024),
        name="message",
    )(rows, coefs, inner, outer)


def stencil_kernel(
    pot_ref, exc_ref, coef_ref, inner_ref, outer_ref, ihigh_ref, ilow_ref, invz_ref, invy_ref,
    out_ref, line_ref, zhigh_ref, zlow_ref, yhigh_ref, ylow_ref,
    pad_ref, dy_ref, high_ref, low_ref, invz_v, invy_v, sems,
):
    nz, ny, nx = pot_ref.shape
    half = nx // 2
    loads = [
        pltpu.make_async_copy(invz_ref, invz_v, sems.at[0]),
        pltpu.make_async_copy(invy_ref, invy_v, sems.at[1]),
    ]
    for copy in loads:
        copy.start()
    below, above = ordered(lax.axis_index("gz") % 2, inner_ref[...], outer_ref[...])
    nothing = jnp.zeros((1, nx), jnp.float32)
    for z in range(nz + 2):
        plane = below if z == 0 else above if z == nz + 1 else pot_ref[z - 1]
        pad_ref[z, 8 : 8 + ny] = plane
        pad_ref[z, 7:8] = nothing
        pad_ref[z, 8 + ny : 9 + ny] = nothing
        dy_ref[z] = pad_ref[z, 9 : 9 + ny] - pad_ref[z, 7 : 7 + ny]
        line_ref[z : z + 1] = plane[ny - 1 :]
    row = lax.broadcasted_iota(jnp.int32, (8, nx), 0)
    first = lax.broadcasted_iota(jnp.int32, (half, 2 * ny), 1) < ny
    matrix = ihigh_ref[...], ilow_ref[...]
    blocks = ny // 8
    for z in range(nz):
        parts = []
        for b in range(blocks):
            rows = slice(8 * b, 8 * b + 8)
            inside = slice(8 * b + 8, 8 * b + 16)
            mixed_xy = lane_difference(dy_ref[z + 1, rows])
            mixed_xz = lane_difference(pad_ref[z + 2, inside] - pad_ref[z, inside])
            mixed_yz = dy_ref[z + 2, rows] - dy_ref[z, rows]
            parts.append(
                exc_ref[z, rows]
                + (
                    coef_ref[0, b : b + 1] * mixed_xy
                    + coef_ref[1, b : b + 1] * mixed_xz
                    + coef_ref[2, b : b + 1] * mixed_yz
                )
            )
        middle, last = parts[blocks // 2], parts[-1]
        parts[0] = jnp.where(row == 0, 0.0, parts[0])
        parts[blocks // 2] = jnp.where(row == 0, last[7:8], middle)
        parts[-1] = jnp.where(row == 7, middle[0:1], last)
        for b in range(0, blocks, 2):
            rows = slice(z * ny + 8 * b, z * ny + 8 * b + 16)
            high_ref[rows], low_ref[rows] = split(jnp.concatenate(parts[b : b + 2], axis=0))
        if z % 2 == 1:
            rows = slice((z - 1) * ny, (z + 1) * ny)
            solved = product(matrix, (high_ref[rows], low_ref[rows]), NT)
            lower, upper = solved[:half], solved[half:]
            out_ref[:, z - 1, :] = jnp.where(first, lower, pltpu.roll(upper, ny, 1))
            out_ref[:, z, :] = jnp.where(first, pltpu.roll(lower, ny, 1), upper)
    for copy in loads:
        copy.wait()
    zhigh_ref[...], zlow_ref[...] = split(invz_v[...])
    width = invy_v.shape[1]
    invy = invy_v[...]
    slot = lax.broadcasted_iota(jnp.int32, invy.shape, 1) % ny
    move = ny // 2 - 1
    yhigh_ref[...], ylow_ref[...] = split(
        jnp.where(
            slot == 0,
            pltpu.roll(invy, width - ny, 1),
            jnp.where(
                slot == ny // 2,
                pltpu.roll(invy, width - move, 1),
                jnp.where(slot == ny - 1, pltpu.roll(invy, move, 1), invy),
            ),
        )
    )


def stencil(potential, excited, coefs, inner, outer, inv_high, inv_low, inverse_z, inverse_y):
    nz, ny, nx = potential.shape
    return pl.pallas_call(
        stencil_kernel,
        in_specs=[VMEM] * 7 + [HBM] * 2,
        out_specs=[VMEM] * 6,
        out_shape=[
            pltpu.VMEM((nx // 2, nz, 2 * ny), jnp.float32),
            pltpu.VMEM((nz + 2, nx), jnp.float32),
        ]
        + [pltpu.VMEM(inverse_z.shape, jnp.bfloat16)] * 2
        + [pltpu.VMEM(inverse_y.shape, jnp.bfloat16)] * 2,
        scratch_shapes=[
            pltpu.VMEM((nz + 2, ny + 16, nx), jnp.float32),
            pltpu.VMEM((nz + 2, ny, nx), jnp.float32),
            pltpu.VMEM((nz * ny, nx), jnp.bfloat16),
            pltpu.VMEM((nz * ny, nx), jnp.bfloat16),
            pltpu.VMEM(inverse_z.shape, jnp.float32),
            pltpu.VMEM(inverse_y.shape, jnp.float32),
            pltpu.SemaphoreType.DMA((2,)),
        ],
        compiler_params=pltpu.CompilerParams(vmem_limit_bytes=20 * 1024 * 1024),
        cost_estimate=pl.CostEstimate(
            flops=6 * nz * ny * nx * nx, bytes_accessed=24 * nz * ny * nx, transcendentals=0
        ),
        name="stencil",
    )(potential, excited, coefs, inner, outer, inv_high, inv_low, *pinned(inverse_z, inverse_y))


def patch_kernel(
    in_ref, line_ref, coef_ref, sent_ref, ihigh_ref, ilow_ref, out_ref, rhs_ref, dy_ref
):
    half, nz, width = in_ref.shape
    ny = width // 2
    pads = nz + 2
    keep = jnp.where(lax.axis_index("gy") == lax.axis_size("gy") - 1, 0.0, 1.0)
    inside = slice(1, nz + 1)
    row = slice(coef_ref.shape[1] - 1, coef_ref.shape[1])
    dy_ref[0:pads] = sent_ref[nz : nz + pads] * keep
    last = coef_ref[0, row] * lane_difference(dy_ref[inside]) + coef_ref[2, row] * (
        dy_ref[2:pads] - dy_ref[0:nz]
    )
    dy_ref[0:pads] = line_ref[...] * keep
    end = nz + pads
    extra = sent_ref[0:nz] - (
        sent_ref[end : end + 1] * lane_difference(dy_ref[inside])
        + sent_ref[end + 1 : end + 2] * (dy_ref[2:pads] - dy_ref[0:nz])
    )
    rhs_ref[...] = jnp.zeros_like(rhs_ref)
    rhs_ref[0:nz] = extra
    rhs_ref[ny // 2 : ny // 2 + nz] = last
    solved = product((ihigh_ref[...], ilow_ref[...]), split(rhs_ref[...]), NT)
    lane = lax.broadcasted_iota(jnp.int32, (half, width), 1)
    both = jnp.where(lane < ny, solved[:half], pltpu.roll(solved[half:], ny, 1))
    for z in range(nz):
        moved = pltpu.roll(both, width - z, 1) if z else both
        out_ref[:, z, :] = in_ref[:, z, :] + jnp.where(lane % (ny // 2) == 0, moved, 0.0)


def patch(tiles, line, coefs, sent, inv_high, inv_low):
    half, nz, width = tiles.shape
    nx = 2 * half
    return pl.pallas_call(
        patch_kernel,
        in_specs=[VMEM] * 6,
        out_specs=VMEM,
        out_shape=pltpu.VMEM(tiles.shape, jnp.float32),
        scratch_shapes=[
            pltpu.VMEM((width, nx), jnp.float32),
            pltpu.VMEM((16, nx), jnp.float32),
        ],
        compiler_params=pltpu.CompilerParams(vmem_limit_bytes=16 * 1024 * 1024),
        cost_estimate=pl.CostEstimate(
            flops=6 * width * nx * nx, bytes_accessed=8 * half * nz * width, transcendentals=0
        ),
        name="patch",
    )(tiles, line, coefs, sent, inv_high, inv_low)


def plane_kernel(
    in_ref, zhigh_ref, zlow_ref, yhigh_ref, ylow_ref, out_ref, high_ref, low_ref
):
    slabs, blocks, depth, width = in_ref.shape
    half = width // 2
    rows = slabs * depth
    matz = zhigh_ref[...], zlow_ref[...]
    first = lax.broadcasted_iota(jnp.int32, (rows, width), 1) < half
    for b in range(0, blocks, 2):
        pair = []
        for k in (b, b + 1):
            pair.append(in_ref[:, k].reshape(rows, width))
        solved = product(matz, split(jnp.concatenate(pair, axis=1)), NN)
        left, right = solved[:, :width], solved[:, width:]
        columns = slice(b * half, (b + 2) * half)
        high_ref[:rows, columns], low_ref[:rows, columns] = split(
            jnp.where(first, left, pltpu.roll(right, half, 1))
        )
        high_ref[rows:, columns], low_ref[rows:, columns] = split(
            jnp.where(first, pltpu.roll(left, half, 1), right)
        )
    for b in range(0, blocks, 2):
        columns = slice(b * half, (b + 2) * half)
        solved = product(
            (high_ref[...], low_ref[...]), (yhigh_ref[columns], ylow_ref[columns]), NT
        )
        one, two = solved[:rows], solved[rows:]
        out_ref[:, b] = jnp.where(first, one, pltpu.roll(two, half, 1)).reshape(slabs, depth, width)
        out_ref[:, b + 1] = jnp.where(first, pltpu.roll(one, half, 1), two).reshape(
            slabs, depth, width
        )


def plane_solve(planes, *matrices):
    slabs, blocks, depth, width = planes.shape
    nz, ny = matrices[0].shape[0], matrices[-1].shape[0]
    return pl.pallas_call(
        plane_kernel,
        in_specs=[VMEM] * 5,
        out_specs=VMEM,
        out_shape=jax.ShapeDtypeStruct(planes.shape, jnp.float32),
        scratch_shapes=[pltpu.VMEM((2 * nz, ny), jnp.bfloat16)] * 2,
        compiler_params=pltpu.CompilerParams(vmem_limit_bytes=16 * 1024 * 1024),
        cost_estimate=pl.CostEstimate(
            flops=12 * nz * ny * (nz + ny), bytes_accessed=16 * nz * ny, transcendentals=0
        ),
        name="plane_solve",
    )(planes, *matrices)


def unpack_kernel(in_ref, out_ref, turned_ref, sems):
    sources, depth, width = in_ref.shape
    ny = width // 2
    copies = []
    for z in range(depth):
        turned = in_ref[:, z, :].T
        turned_ref[z, :, :sources] = turned[:ny]
        turned_ref[z, :, sources:] = turned[ny:]
        copies.append(pltpu.make_async_copy(turned_ref.at[z], out_ref.at[z], sems.at[z]))
        copies[-1].start()
    for copy in copies:
        copy.wait()


def unpack(tiles):
    sources, depth, width = tiles.shape
    shape = (depth, width // 2, 2 * sources)
    return pl.pallas_call(
        unpack_kernel,
        in_specs=[VMEM],
        out_specs=HBM,
        out_shape=jax.ShapeDtypeStruct(shape, jnp.float32),
        scratch_shapes=[pltpu.VMEM(shape, jnp.float32), pltpu.SemaphoreType.DMA((depth,))],
        cost_estimate=pl.CostEstimate(
            flops=0, bytes_accessed=8 * sources * depth * width, transcendentals=0
        ),
        name="unpack",
    )(pltpu.with_memory_space_constraint(tiles, pltpu.VMEM))


def swaps(axis, inner, outer):
    count = lax.axis_size(axis)

    def both(first):
        pairs = [(i, i + 1) for i in range(first, count - 1, 2)]
        return pairs + [(j, i) for i, j in pairs]

    return lax.ppermute(outer, axis, both(1)), lax.ppermute(inner, axis, both(0))


def shards(
    potential,
    fast_gate,
    slow_gate,
    tissue,
    region_ids,
    fibre_table,
    inverse_x,
    inverse_z,
    inverse_y,
):
    inner, outer = faces(potential)
    z_outer, z_inner = swaps("gz", inner, outer)
    held, excited, rows, coefs, inv_high, inv_low, new_fast, new_slow = ionic(
        fibre_table.T, potential, fast_gate, slow_gate, tissue, region_ids[0], inverse_x
    )
    z_outer, z_inner, rows, coefs = lax.optimization_barrier((z_outer, z_inner, rows, coefs))
    count = lax.axis_size("gy")
    sent = lax.ppermute(
        message(rows, coefs, z_inner, z_outer), "gy", [((i + 1) % count, i) for i in range(count)]
    )
    tiles, line, *matrices = stencil(
        held, excited, coefs, z_inner, z_outer, inv_high, inv_low, inverse_z, inverse_y
    )
    tiles = patch(tiles, line, coefs, sent, inv_high, inv_low)
    axes = ("gz", "gy")
    planes = lax.all_to_all(tiles, axes, split_axis=0, concat_axis=0, tiled=True)
    slabs, blocks = lax.axis_size("gz"), lax.axis_size("gy")
    solved = plane_solve(planes.reshape((slabs, blocks) + planes.shape[1:]), *matrices)
    back = lax.all_to_all(
        solved.reshape(planes.shape), axes, split_axis=0, concat_axis=0, tiled=True
    )
    return (unpack(back), new_fast, new_slow)


def solution(mesh):
    return jax.shard_map(
        shards,
        mesh=mesh,
        in_specs=(
            P("gz", "gy", None),
            P("gz", "gy", None),
            P("gz", "gy", None),
            P("gz", "gy", None),
            P("gz", "gy", None),
            P(),
            P(),
            P(),
            P(),
        ),
        out_specs=(P("gz", "gy", None), P("gz", "gy", None), P("gz", "gy", None)),
        check_vma=False,
    )
```

time: 111 us -> 106 us (0.955)
  blocking collectives: 84.9 us -> 79.6 us
  other arithmetic: 1.72 us -> 0 us
  Pallas kernels: 13.1 us -> 14.8 us
  starting transfers between devices: 7.95 us -> 9.49 us
    ppermute x0 -> x1, starting transfers between devices: none -> 5.47 us  [shards(): lax.ppermute(message(rows, coefs, z_inner, z_outer), 'gy', [((i + 1) % co...]
    all_to_all x1, blocking collectives: 47.5 us -> 42.3 us  [shards(): lax.all_to_all(tiles, axes, split_axis=0, concat_axis=0, tiled=True)]
    ppermute x2 -> x1, starting transfers between devices: 5.39 us -> 2.11 us  [swaps(): lax.ppermute(inner, axis, both(0))]
    select_n x3 -> x0, other arithmetic: 1.72 us -> none  [the longest x1 1.69 us: shards(): jnp.where(odd == 1, first, last)]
    pallas_call x5 -> x7, Pallas kernels: 13.1 us -> 14.8 us  [the longest x1 4.41 us: ionic(): pl.pallas_call(ionic_kernel, in_specs=[HBM] * 7, out_specs=[VMEM] * 6 + [...]
    ppermute x2 -> x1, starting transfers between devices: 2.56 us -> 1.92 us  [swaps(): lax.ppermute(outer, axis, both(1))]
  transfers between devices with their start and end apart: 4 -> 3, of which waited for: 0 -> 0; matrix products, arithmetic and copies ran while one was open for 0% -> 0% of each run, Pallas kernels for 5% -> 8%
where the time goes in v3:
time: 106 us; the launch traced here: 105 us
  blocking collectives  79.6 us (75%)
  Pallas kernels  14.8 us (14%)
  starting transfers between devices  9.49 us (9%)
    all_to_all x1, blocking collectives, shards(): lax.all_to_all(tiles, axes, split_axis=0, concat_axis=0, tiled=True)  42.3 us
    all_to_all x1, blocking collectives, shards(): lax.all_to_all(solved.reshape(planes.shape), axes, split_axis=0, concat_a...  37.3 us
    ppermute x1, starting transfers between devices, shards(): lax.ppermute(message(rows, coefs, z_inner, z_outer), 'gy', [((i + 1) % co...  5.47 us
    pallas_call x1, Pallas kernels, ionic(): pl.pallas_call(ionic_kernel, in_specs=[HBM] * 7, out_specs=[VMEM] * 6 + [...  4.41 us
    pallas_call x1, Pallas kernels, stencil(): pl.pallas_call(stencil_kernel, in_specs=[VMEM] * 7 + [HBM] * 2, out_specs...  3.85 us
    pallas_call x1, Pallas kernels, plane_solve(): pl.pallas_call(plane_kernel, in_specs=[VMEM] * 5, out_specs=VMEM, out_sha...  2.31 us
  transfers between devices with their start and end apart: 3, of which 0 were waited for; matrix products, arithmetic and copies ran while one was open for 0% of the time, Pallas kernels for 8%

profile of v3, /device:TPU:32, one launch (start us, length us, event | category | flops | bytes accessed | tf_op | source)
XLA Modules:
  0.0 104.6 jit_solution(6129450993552344753)
XLA Ops:
  0.6 1.0 faces.1
  1.6 1.9 %collective-permute-start = (f32[64,512]{1,0:T(8,128)S(1)}, f32[64,512]{1,0:T(8,128)S(1)}, u32[]{:S(2)}, u32[]{:S(2)}) collective-permute-start(f32[64,512]{1,0:T(8,128)S(1)} %get-tuple-element.25), channel_id=1, source_target_pairs={{8,16},{24,32},{40,48},{56,64},{72,80},{88,96},{104,112},{120,128}... | collective-permute-start | bytes 393224 | tf_op jit(solution)/shard_map/ppermute | solution.py:501
  3.6 2.1 %collective-permute-start.1 = (f32[64,512]{1,0:T(8,128)S(1)}, f32[64,512]{1,0:T(8,128)S(1)}, u32[]{:S(2)}, u32[]{:S(2)}) collective-permute-start(f32[64,512]{1,0:T(8,128)S(1)} %get-tuple-element.26), channel_id=1, source_target_pairs={{0,8},{16,24},{32,40},{48,56},{64,72},{80,88},{96,104},{112,120},{... | collective-permute-start | bytes 393224 | tf_op jit(solution)/shard_map/ppermute | solution.py:501
  5.7 4.4 %ionic.1 = (f32[8,64,512]{2,1,0:T(8,128)S(1)}, f32[8,64,512]{2,1,0:T(8,128)S(1)}, f32[24,512]{1,0:T(8,128)S(1)}, f32[3,8,512]{2,1,0:T(8,128)S(1)}, bf16[512,512]...) custom-call(f32[3,8]{1,0:T(4,128)} %bitcast.7, ...), custom_call_target="tpu_custom_call" | custom-call | flops 10485760 | bytes 7340032 | tf_op jit(solution)/shard_map/ionic/pallas_call | solution.py:147
  10.1 0.0 collective-permute-done.outer_ref
  10.1 0.0 collective-permute-done.1.inner_ref
  10.1 0.1 message.1
  10.2 5.5 %collective-permute-start.2 = (f32[24,512]{1,0:T(8,128)S(1)}, f32[24,512]{1,0:T(8,128)S(1)}, u32[]{:S(2)}, u32[]{:S(2)}) collective-permute-start(f32[24,512]{1,0:T(8,128)S(1)} %message.1), channel_id=1, source_target_pairs={{1,0},{2,1},{3,2},{4,3},{5,4},{6,5},{7,6},{0,7},{9,8},{10,9},{11,1... | collective-permute-start | bytes 147464 | tf_op jit(solution)/shard_map/ppermute | solution.py:522
  15.7 3.9 %stencil.1 = (f32[256,8,128]{2,1,0:T(8,128)S(1)}, f32[10,512]{1,0:T(8,128)S(1)}, bf16[256,256]{1,0:T(8,128)(2,1)S(1)}, bf16[256,256]{1,0:T(8,128)(2,1)S(1)}, bf1...) custom-call(f32[8,64,512]{2,1,0:T(8,128)S(1)} %get-tuple-element.23.pot_ref, ...), custom_call_target="tpu_custom_call" | custom-call | flops 805306368 | bytes 6291456 | tf_op jit(solution)/shard_map/stencil/pallas_call | solution.py:337
  19.6 0.0 collective-permute-done.2.sent_ref
  19.6 1.7 %patch.1 = f32[256,8,128]{2,1,0:T(8,128)S(1)} custom-call(f32[256,8,128]{2,1,0:T(8,128)S(1)} %get-tuple-element.34.in_ref, f32[10,512]{1,0:T(8,128)S(1)} %get-tuple-element.35.line_ref, f32[3,8,512]{2,1,0:T(8,128)S(1)} %get-tuple-element.29.coef_ref, f32[24,512]{1,0:T(8,128)S(1)} %collective-permute-done.2.sent_ref, ...), custom_call_target="tpu_custom_call" | custom-call | flops 201326592 | bytes 2097152 | tf_op jit(solution)/shard_map/patch/pallas_call | solution.py:397
  21.3 42.3 %all_to_all.10 = f32[256,8,128]{2,1,0:T(8,128)S(1)} all-to-all(f32[256,8,128]{2,1,0:T(8,128)S(1)} %patch.1), channel_id=1, replica_groups=mesh['gz'=32,'gy'=8] {'gz','gy'}, dimensions={0} | all-to-all | bytes 2097152 | tf_op jit(solution)/shard_map/all_to_all | solution.py:530
  63.6 2.3 %plane_solve.1 = f32[32,8,8,128]{3,2,1,0:T(8,128)S(1)} custom-call(f32[32,8,8,128]{3,2,1,0:T(8,128)S(1)} %bitcast.4, bf16[256,256]{1,0:T(8,128)(2,1)S(1)} %get-tuple-element.37.zhigh_ref, bf16[256,256]{1,0:T(8,128)(2,1)S(1)} %get-tuple-element.38.zlow_ref, bf16[512,512]{1,0:T(8,128)(2,1)S(1)} %get-tuple-element.39.yhigh_ref, ...), custom_call_target="tpu_custom_call" | custom-call | flops 1207959552 | bytes 2097152 | tf_op jit(solution)/shard_map/plane_solve/pallas_call | solution.py:450
  65.9 37.3 %all_to_all.11.in_ref = f32[256,8,128]{2,1,0:T(8,128)S(1)} all-to-all(f32[256,8,128]{2,1,0:T(8,128)S(1)} %bitcast.5), channel_id=1, replica_groups=mesh['gz'=32,'gy'=8] {'gz','gy'}, dimensions={0} | all-to-all | bytes 2097152 | tf_op jit(solution)/shard_map/all_to_all | solution.py:533
  103.2 1.4 %unpack.1 = f32[8,64,512]{2,1,0:T(8,128)} custom-call(f32[256,8,128]{2,1,0:T(8,128)S(1)} %all_to_all.11.in_ref), custom_call_target="tpu_custom_call" | custom-call | bytes 2097152 | tf_op jit(solution)/shard_map/unpack/pallas_call | solution.py:481
Async XLA Ops:
  1.6 8.5 %collective-permute-start = (f32[64,512]{1,0:T(8,128)S(1)}, f32[64,512]{1,0:T(8,128)S(1)}, u32[]{:S(2)}, u32[]{:S(2)}) collective-permute-start(f32[64,512]{1,0:T(8,128)S(1)} %get-tuple-element.25), channel_id=1, source_target_pairs={{8,16},{24,32},{40,48},{56,64},{72,80},{88,96},{104,112},{120,128}... | collective-permute-start | bytes 393224 | tf_op jit(solution)/shard_map/ppermute | solution.py:501
  3.6 6.5 %collective-permute-start.1 = (f32[64,512]{1,0:T(8,128)S(1)}, f32[64,512]{1,0:T(8,128)S(1)}, u32[]{:S(2)}, u32[]{:S(2)}) collective-permute-start(f32[64,512]{1,0:T(8,128)S(1)} %get-tuple-element.26), channel_id=1, source_target_pairs={{0,8},{16,24},{32,40},{48,56},{64,72},{80,88},{96,104},{112,120},{... | collective-permute-start | bytes 393224 | tf_op jit(solution)/shard_map/ppermute | solution.py:501
  10.2 9.3 %collective-permute-start.2 = (f32[24,512]{1,0:T(8,128)S(1)}, f32[24,512]{1,0:T(8,128)S(1)}, u32[]{:S(2)}, u32[]{:S(2)}) collective-permute-start(f32[24,512]{1,0:T(8,128)S(1)} %message.1), channel_id=1, source_target_pairs={{1,0},{2,1},{3,2},{4,3},{5,4},{6,5},{7,6},{0,7},{9,8},{10,9},{11,1... | collective-permute-start | bytes 147464 | tf_op jit(solution)/shard_map/ppermute | solution.py:522

commit v4 on v3

--- a/solution.py
+++ b/solution.py
@@ -78,8 +78,7 @@
 def ionic_kernel(
     table_ref, pot_ref, fast_ref, slow_ref, tissue_ref, region_ref, inv_ref,
     potc_ref, exc_ref, rows_ref, coef_ref, ihigh_ref, ilow_ref, nfast_ref, nslow_ref,
-    fast_v, slow_v, tissue_v, region_v, inv_v, nfast_v, nslow_v, table_s,
-    in_sems, out_sems, sems,
+    fast_v, slow_v, tissue_v, region_v, inv_v, table_s, in_sems, sems,
 ):
     nz, ny, nx = pot_ref.shape
     extra = [
@@ -92,13 +91,6 @@
         [
             pltpu.make_async_copy(source.at[z], target.at[z], in_sems.at[k, z])
             for k, (source, target) in enumerate(pairs)
-        ]
-        for z in range(nz)
-    ]
-    stores = [
-        [
-            pltpu.make_async_copy(source.at[z], target.at[z], out_sems.at[k, z])
-            for k, (source, target) in enumerate(((nfast_v, nfast_ref), (nslow_v, nslow_ref)))
         ]
         for z in range(nz)
     ]
@@ -123,10 +115,8 @@
                 jnp.where(p >= vgate_crit, decay(vopen_high), decay(vopen_low)),
             )
             keep_slow = jnp.where(active, decay(wclose_tau), decay(wopen_tau))
-            nfast_v[rows] = jnp.where(living, target + (v - target) * keep_fast, v)
-            nslow_v[rows] = jnp.where(living, target + (w - target) * keep_slow, w)
-        for copy in stores[z]:
-            copy.start()
+            nfast_ref[rows] = jnp.where(living, target + (v - target) * keep_fast, v)
+            nslow_ref[rows] = jnp.where(living, target + (w - target) * keep_slow, w)
         for k, line in enumerate((potc_ref[z, 0:1], potc_ref[z, 1:2], exc_ref[z, 0:1])):
             rows_ref[k * nz + z : k * nz + z + 1] = line
     for copy in extra:
@@ -134,20 +124,16 @@
     for column, coef in enumerate(coefficients(table_s, region_v, nx)):
         coef_ref[column] = coef
     ihigh_ref[...], ilow_ref[...] = split(inv_v[...])
-    for group in stores:
-        for copy in group:
-            copy.wait()
 
 
 def ionic(table, potential, fast_gate, slow_gate, tissue, region, inverse_x):
     nz, ny, nx = potential.shape
-    shape = jax.ShapeDtypeStruct((nz, ny, nx), jnp.float32)
     field = pltpu.VMEM((nz, ny, nx), jnp.float32)
     part = pltpu.VMEM((nx, nx), jnp.bfloat16)
     return pl.pallas_call(
         ionic_kernel,
         in_specs=[HBM] * 7,
-        out_specs=[VMEM] * 6 + [HBM] * 2,
+        out_specs=[VMEM] * 8,
         out_shape=[
             field,
             field,
@@ -155,8 +141,8 @@
             pltpu.VMEM((3, ny // 8, nx), jnp.float32),
             part,
             part,
-            shape,
-            shape,
+            field,
+            field,
         ],
         scratch_shapes=[
             field,
@@ -164,11 +150,8 @@
             pltpu.VMEM((nz, ny, nx), jnp.int32),
             pltpu.VMEM(region.shape, jnp.int32),
             pltpu.VMEM((nx, nx), jnp.float32),
-            field,
-            field,
             pltpu.SMEM(table.shape, jnp.float32),
             pltpu.SemaphoreType.DMA((4, nz)),
-            pltpu.SemaphoreType.DMA((2, nz)),
             pltpu.SemaphoreType.DMA((3,)),
         ],
         compiler_params=pltpu.CompilerParams(vmem_limit_bytes=16 * 1024 * 1024),
@@ -259,7 +242,8 @@
 
 def stencil_kernel(
     pot_ref, exc_ref, coef_ref, inner_ref, outer_ref, ihigh_ref, ilow_ref, invz_ref, invy_ref,
-    out_ref, line_ref, zhigh_ref, zlow_ref, yhigh_ref, ylow_ref,
+    nfast_v, nslow_v,
+    out_ref, line_ref, zhigh_ref, zlow_ref, yhigh_ref, ylow_ref, nfast_ref, nslow_ref,
     pad_ref, dy_ref, high_ref, low_ref, invz_v, invy_v, sems,
 ):
     nz, ny, nx = pot_ref.shape
@@ -268,7 +252,11 @@
         pltpu.make_async_copy(invz_ref, invz_v, sems.at[0]),
         pltpu.make_async_copy(invy_ref, invy_v, sems.at[1]),
     ]
-    for copy in loads:
+    stores = [
+        pltpu.make_async_copy(nfast_v, nfast_ref, sems.at[2]),
+        pltpu.make_async_copy(nslow_v, nslow_ref, sems.at[3]),
+    ]
+    for copy in loads + stores:
         copy.start()
     below, above = ordered(lax.axis_index("gz") % 2, inner_ref[...], outer_ref[...])
     nothing = jnp.zeros((1, nx), jnp.float32)
@@ -299,51 +287,47 @@
                     + coef_ref[2, b : b + 1] * mixed_yz
                 )
             )
-        middle, last = parts[blocks // 2], parts[-1]
         parts[0] = jnp.where(row == 0, 0.0, parts[0])
-        parts[blocks // 2] = jnp.where(row == 0, last[7:8], middle)
-        parts[-1] = jnp.where(row == 7, middle[0:1], last)
         for b in range(0, blocks, 2):
             rows = slice(z * ny + 8 * b, z * ny + 8 * b + 16)
             high_ref[rows], low_ref[rows] = split(jnp.concatenate(parts[b : b + 2], axis=0))
-        if z % 2 == 1:
-            rows = slice((z - 1) * ny, (z + 1) * ny)
+        if z % 4 == 3:
+            rows = slice((z - 3) * ny, (z + 1) * ny)
             solved = product(matrix, (high_ref[rows], low_ref[rows]), NT)
-            lower, upper = solved[:half], solved[half:]
-            out_ref[:, z - 1, :] = jnp.where(first, lower, pltpu.roll(upper, ny, 1))
-            out_ref[:, z, :] = jnp.where(first, pltpu.roll(lower, ny, 1), upper)
+            for k in range(2):
+                columns = slice(2 * k * ny, 2 * (k + 1) * ny)
+                lower, upper = solved[:half, columns], solved[half:, columns]
+                at = z - 3 + 2 * k
+                out_ref[:, at, :] = jnp.where(first, lower, pltpu.roll(upper, ny, 1))
+                out_ref[:, at + 1, :] = jnp.where(first, pltpu.roll(lower, ny, 1), upper)
     for copy in loads:
         copy.wait()
     zhigh_ref[...], zlow_ref[...] = split(invz_v[...])
     width = invy_v.shape[1]
     invy = invy_v[...]
-    slot = lax.broadcasted_iota(jnp.int32, invy.shape, 1) % ny
-    move = ny // 2 - 1
+    column = lax.broadcasted_iota(jnp.int32, invy.shape, 1)
     yhigh_ref[...], ylow_ref[...] = split(
-        jnp.where(
-            slot == 0,
-            pltpu.roll(invy, width - ny, 1),
-            jnp.where(
-                slot == ny // 2,
-                pltpu.roll(invy, width - move, 1),
-                jnp.where(slot == ny - 1, pltpu.roll(invy, move, 1), invy),
-            ),
-        )
-    )
-
-
-def stencil(potential, excited, coefs, inner, outer, inv_high, inv_low, inverse_z, inverse_y):
+        jnp.where(column % ny == 0, pltpu.roll(invy, width - ny, 1), invy)
+    )
+    for copy in stores:
+        copy.wait()
+
+
+def stencil(
+    potential, excited, coefs, inner, outer, inv_high, inv_low, inverse_z, inverse_y, *gates
+):
     nz, ny, nx = potential.shape
     return pl.pallas_call(
         stencil_kernel,
-        in_specs=[VMEM] * 7 + [HBM] * 2,
-        out_specs=[VMEM] * 6,
+        in_specs=[VMEM] * 7 + [HBM] * 2 + [VMEM] * 2,
+        out_specs=[VMEM] * 6 + [HBM] * 2,
         out_shape=[
             pltpu.VMEM((nx // 2, nz, 2 * ny), jnp.float32),
             pltpu.VMEM((nz + 2, nx), jnp.float32),
         ]
         + [pltpu.VMEM(inverse_z.shape, jnp.bfloat16)] * 2
-        + [pltpu.VMEM(inverse_y.shape, jnp.bfloat16)] * 2,
+        + [pltpu.VMEM(inverse_y.shape, jnp.bfloat16)] * 2
+        + [jax.ShapeDtypeStruct((nz, ny, nx), jnp.float32)] * 2,
         scratch_shapes=[
             pltpu.VMEM((nz + 2, ny + 16, nx), jnp.float32),
             pltpu.VMEM((nz + 2, ny, nx), jnp.float32),
@@ -351,14 +335,17 @@
             pltpu.VMEM((nz * ny, nx), jnp.bfloat16),
             pltpu.VMEM(inverse_z.shape, jnp.float32),
             pltpu.VMEM(inverse_y.shape, jnp.float32),
-            pltpu.SemaphoreType.DMA((2,)),
+            pltpu.SemaphoreType.DMA((4,)),
         ],
-        compiler_params=pltpu.CompilerParams(vmem_limit_bytes=20 * 1024 * 1024),
+        compiler_params=pltpu.CompilerParams(vmem_limit_bytes=24 * 1024 * 1024),
         cost_estimate=pl.CostEstimate(
-            flops=6 * nz * ny * nx * nx, bytes_accessed=24 * nz * ny * nx, transcendentals=0
+            flops=6 * nz * ny * nx * nx, bytes_accessed=32 * nz * ny * nx, transcendentals=0
         ),
         name="stencil",
-    )(potential, excited, coefs, inner, outer, inv_high, inv_low, *pinned(inverse_z, inverse_y))
+    )(
+        potential, excited, coefs, inner, outer, inv_high, inv_low,
+        *pinned(inverse_z, inverse_y), *gates,
+    )
 
 
 def patch_kernel(
@@ -381,14 +368,18 @@
         + sent_ref[end + 1 : end + 2] * (dy_ref[2:pads] - dy_ref[0:nz])
     )
     rhs_ref[...] = jnp.zeros_like(rhs_ref)
-    rhs_ref[0:nz] = extra
-    rhs_ref[ny // 2 : ny // 2 + nz] = last
+    for z in range(nz):
+        rhs_ref[2 * z : 2 * z + 1] = extra[z : z + 1]
+        rhs_ref[ny - 1 + 2 * z : ny + 2 * z] = last[z : z + 1]
     solved = product((ihigh_ref[...], ilow_ref[...]), split(rhs_ref[...]), NT)
     lane = lax.broadcasted_iota(jnp.int32, (half, width), 1)
-    both = jnp.where(lane < ny, solved[:half], pltpu.roll(solved[half:], ny, 1))
+    even = lane % 2 == 0
+    lower = ((lane < ny // 2) & even) | ((lane >= ny // 2) & (lane < ny + ny // 2) & ~even)
+    both = jnp.where(lower, solved[:half], pltpu.roll(solved[half:], ny, 1))
+    ends = (lane % ny == 0) | (lane % ny == ny - 1)
     for z in range(nz):
-        moved = pltpu.roll(both, width - z, 1) if z else both
-        out_ref[:, z, :] = in_ref[:, z, :] + jnp.where(lane % (ny // 2) == 0, moved, 0.0)
+        moved = pltpu.roll(both, width - 2 * z, 1) if z else both
+        out_ref[:, z, :] = in_ref[:, z, :] + jnp.where(ends, moved, 0.0)
 
 
 def patch(tiles, line, coefs, sent, inv_high, inv_low):
@@ -432,16 +423,17 @@
         high_ref[rows:, columns], low_ref[rows:, columns] = split(
             jnp.where(first, pltpu.roll(left, half, 1), right)
         )
-    for b in range(0, blocks, 2):
-        columns = slice(b * half, (b + 2) * half)
+    tile = (slabs, depth, width)
+    for start in range(0, blocks, 4):
+        columns = slice(start * half, (start + 4) * half)
         solved = product(
             (high_ref[...], low_ref[...]), (yhigh_ref[columns], ylow_ref[columns]), NT
         )
-        one, two = solved[:rows], solved[rows:]
-        out_ref[:, b] = jnp.where(first, one, pltpu.roll(two, half, 1)).reshape(slabs, depth, width)
-        out_ref[:, b + 1] = jnp.where(first, pltpu.roll(one, half, 1), two).reshape(
-            slabs, depth, width
-        )
+        for b in (start, start + 2):
+            columns = slice((b - start) * half, (b - start + 2) * half)
+            one, two = solved[:rows, columns], solved[rows:, columns]
+            out_ref[:, b] = jnp.where(first, one, pltpu.roll(two, half, 1)).reshape(tile)
+            out_ref[:, b + 1] = jnp.where(first, pltpu.roll(one, half, 1), two).reshape(tile)
 
 
 def plane_solve(planes, *matrices):
@@ -514,7 +506,7 @@
 ):
     inner, outer = faces(potential)
     z_outer, z_inner = swaps("gz", inner, outer)
-    held, excited, rows, coefs, inv_high, inv_low, new_fast, new_slow = ionic(
+    held, excited, rows, coefs, inv_high, inv_low, *gates = ionic(
         fibre_table.T, potential, fast_gate, slow_gate, tissue, region_ids[0], inverse_x
     )
     z_outer, z_inner, rows, coefs = lax.optimization_barrier((z_outer, z_inner, rows, coefs))
@@ -522,8 +514,8 @@
     sent = lax.ppermute(
         message(rows, coefs, z_inner, z_outer), "gy", [((i + 1) % count, i) for i in range(count)]
     )
-    tiles, line, *matrices = stencil(
-        held, excited, coefs, z_inner, z_outer, inv_high, inv_low, inverse_z, inverse_y
+    tiles, line, *matrices, new_fast, new_slow = stencil(
+        held, excited, coefs, z_inner, z_outer, inv_high, inv_low, inverse_z, inverse_y, *gates
     )
     tiles = patch(tiles, line, coefs, sent, inv_high, inv_low)
     axes = ("gz", "gy")

time: 106 us -> 105 us (level)
  Pallas kernels: 14.8 us -> 12.9 us
  blocking collectives: 79.6 us -> 80.7 us
    pallas_call x2, Pallas kernels: 8.26 us -> 7.03 us  [the longest x1 3.68 us: stencil(): pl.pallas_call(stencil_kernel, in_specs=[VMEM] * 7 + [HBM] * 2 + [VMEM] *...]
    all_to_all x1, blocking collectives: 42.3 us -> 43.4 us  [shards(): lax.all_to_all(tiles, axes, split_axis=0, concat_axis=0, tiled=True)]
  transfers between devices with their start and end apart: 3 -> 3, of which waited for: 0 -> 0; matrix products, arithmetic and copies ran while one was open for 0% -> 0% of each run, Pallas kernels for 8% -> 7%
where the time goes in v4:
time: 105 us; the launch traced here: 104 us
  blocking collectives  80.7 us (77%)
  Pallas kernels  12.9 us (12%)
  starting transfers between devices  9.49 us (9%)
    all_to_all x1, blocking collectives, shards(): lax.all_to_all(tiles, axes, split_axis=0, concat_axis=0, tiled=True)  43.4 us
    all_to_all x1, blocking collectives, shards(): lax.all_to_all(solved.reshape(planes.shape), axes, split_axis=0, concat_a...  37.3 us
    ppermute x1, starting transfers between devices, shards(): lax.ppermute(message(rows, coefs, z_inner, z_outer), 'gy', [((i + 1) % co...  5.47 us
    pallas_call x1, Pallas kernels, stencil(): pl.pallas_call(stencil_kernel, in_specs=[VMEM] * 7 + [HBM] * 2 + [VMEM] *...  3.68 us
    pallas_call x1, Pallas kernels, ionic(): pl.pallas_call(ionic_kernel, in_specs=[HBM] * 7, out_specs=[VMEM] * 8, ou...  3.35 us
    ppermute x1, starting transfers between devices, swaps(): lax.ppermute(inner, axis, both(0))  2.11 us
  transfers between devices with their start and end apart: 3, of which 0 were waited for; matrix products, arithmetic and copies ran while one was open for 0% of the time, Pallas kernels for 7%

profile of v4, /device:TPU:32, one launch (start us, length us, event | category | flops | bytes accessed | tf_op | source)
XLA Modules:
  0.0 103.8 jit_solution(4626650256689027874)
XLA Ops:
  0.6 1.0 faces.1
  1.6 1.9 %collective-permute-start = (f32[64,512]{1,0:T(8,128)S(1)}, f32[64,512]{1,0:T(8,128)S(1)}, u32[]{:S(2)}, u32[]{:S(2)}) collective-permute-start(f32[64,512]{1,0:T(8,128)S(1)} %get-tuple-element.27), channel_id=1, source_target_pairs={{8,16},{24,32},{40,48},{56,64},{72,80},{88,96},{104,112},{120,128}... | collective-permute-start | bytes 393224 | tf_op jit(solution)/shard_map/ppermute | solution.py:493
  3.6 2.1 %collective-permute-start.1 = (f32[64,512]{1,0:T(8,128)S(1)}, f32[64,512]{1,0:T(8,128)S(1)}, u32[]{:S(2)}, u32[]{:S(2)}) collective-permute-start(f32[64,512]{1,0:T(8,128)S(1)} %get-tuple-element.28), channel_id=1, source_target_pairs={{0,8},{16,24},{32,40},{48,56},{64,72},{80,88},{96,104},{112,120},{... | collective-permute-start | bytes 393224 | tf_op jit(solution)/shard_map/ppermute | solution.py:493
  5.7 3.4 %ionic.1 = (f32[8,64,512]{2,1,0:T(8,128)S(1)}, f32[8,64,512]{2,1,0:T(8,128)S(1)}, f32[24,512]{1,0:T(8,128)S(1)}, f32[3,8,512]{2,1,0:T(8,128)S(1)}, bf16[512,512]...) custom-call(f32[3,8]{1,0:T(4,128)} %bitcast.7, ...), custom_call_target="tpu_custom_call" | custom-call | flops 10485760 | bytes 7340032 | tf_op jit(solution)/shard_map/ionic/pallas_call | solution.py:133
  9.0 0.0 collective-permute-done.outer_ref
  9.0 0.0 collective-permute-done.1.inner_ref
  9.1 0.1 message.1
  9.2 5.5 %collective-permute-start.2 = (f32[24,512]{1,0:T(8,128)S(1)}, f32[24,512]{1,0:T(8,128)S(1)}, u32[]{:S(2)}, u32[]{:S(2)}) collective-permute-start(f32[24,512]{1,0:T(8,128)S(1)} %message.1), channel_id=1, source_target_pairs={{1,0},{2,1},{3,2},{4,3},{5,4},{6,5},{7,6},{0,7},{9,8},{10,9},{11,1... | collective-permute-start | bytes 147464 | tf_op jit(solution)/shard_map/ppermute | solution.py:514
  14.6 3.7 %stencil.1 = (f32[256,8,128]{2,1,0:T(8,128)S(1)}, f32[10,512]{1,0:T(8,128)S(1)}, bf16[256,256]{1,0:T(8,128)(2,1)S(1)}, bf16[256,256]{1,0:T(8,128)(2,1)S(1)}, bf1...) custom-call(f32[8,64,512]{2,1,0:T(8,128)S(1)} %get-tuple-element.25.pot, ...), custom_call_target="tpu_custom_call" | custom-call | flops 805306368 | bytes 8388608 | tf_op jit(solution)/shard_map/stencil/pallas_call | solution.py:320
  18.3 0.0 collective-permute-done.2.sent_ref
  18.3 1.8 %patch.1 = f32[256,8,128]{2,1,0:T(8,128)S(1)} custom-call(f32[256,8,128]{2,1,0:T(8,128)S(1)} %get-tuple-element.38.in_ref, f32[10,512]{1,0:T(8,128)S(1)} %get-tuple-element.39.line_ref, f32[3,8,512]{2,1,0:T(8,128)S(1)} %get-tuple-element.31.coef_ref, f32[24,512]{1,0:T(8,128)S(1)} %collective-permute-done.2.sent_ref, ...), custom_call_target="tpu_custom_call" | custom-call | flops 201326592 | bytes 2097152 | tf_op jit(solution)/shard_map/patch/pallas_call | solution.py:388
  20.1 43.4 %all_to_all.10 = f32[256,8,128]{2,1,0:T(8,128)S(1)} all-to-all(f32[256,8,128]{2,1,0:T(8,128)S(1)} %patch.1), channel_id=1, replica_groups=mesh['gz'=32,'gy'=8] {'gz','gy'}, dimensions={0} | all-to-all | bytes 2097152 | tf_op jit(solution)/shard_map/all_to_all | solution.py:522
  63.5 1.6 %plane_solve.1 = f32[32,8,8,128]{3,2,1,0:T(8,128)S(1)} custom-call(f32[32,8,8,128]{3,2,1,0:T(8,128)S(1)} %bitcast.4, bf16[256,256]{1,0:T(8,128)(2,1)S(1)} %get-tuple-element.41.zhigh_ref, bf16[256,256]{1,0:T(8,128)(2,1)S(1)} %get-tuple-element.42.zlow_ref, bf16[512,512]{1,0:T(8,128)(2,1)S(1)} %get-tuple-element.43.yhigh_ref, ...), custom_call_target="tpu_custom_call" | custom-call | flops 1207959552 | bytes 2097152 | tf_op jit(solution)/shard_map/plane_solve/pallas_call | solution.py:442
  65.2 37.3 %all_to_all.11.in_ref = f32[256,8,128]{2,1,0:T(8,128)S(1)} all-to-all(f32[256,8,128]{2,1,0:T(8,128)S(1)} %bitcast.5), channel_id=1, replica_groups=mesh['gz'=32,'gy'=8] {'gz','gy'}, dimensions={0} | all-to-all | bytes 2097152 | tf_op jit(solution)/shard_map/all_to_all | solution.py:525
  102.5 1.4 %unpack.1 = f32[8,64,512]{2,1,0:T(8,128)} custom-call(f32[256,8,128]{2,1,0:T(8,128)S(1)} %all_to_all.11.in_ref), custom_call_target="tpu_custom_call" | custom-call | bytes 2097152 | tf_op jit(solution)/shard_map/unpack/pallas_call | solution.py:473
Async XLA Ops:
  1.6 7.4 %collective-permute-start = (f32[64,512]{1,0:T(8,128)S(1)}, f32[64,512]{1,0:T(8,128)S(1)}, u32[]{:S(2)}, u32[]{:S(2)}) collective-permute-start(f32[64,512]{1,0:T(8,128)S(1)} %get-tuple-element.27), channel_id=1, source_target_pairs={{8,16},{24,32},{40,48},{56,64},{72,80},{88,96},{104,112},{120,128}... | collective-permute-start | bytes 393224 | tf_op jit(solution)/shard_map/ppermute | solution.py:493
  3.6 5.5 %collective-permute-start.1 = (f32[64,512]{1,0:T(8,128)S(1)}, f32[64,512]{1,0:T(8,128)S(1)}, u32[]{:S(2)}, u32[]{:S(2)}) collective-permute-start(f32[64,512]{1,0:T(8,128)S(1)} %get-tuple-element.28), channel_id=1, source_target_pairs={{0,8},{16,24},{32,40},{48,56},{64,72},{80,88},{96,104},{112,120},{... | collective-permute-start | bytes 393224 | tf_op jit(solution)/shard_map/ppermute | solution.py:493
  9.2 9.2 %collective-permute-start.2 = (f32[24,512]{1,0:T(8,128)S(1)}, f32[24,512]{1,0:T(8,128)S(1)}, u32[]{:S(2)}, u32[]{:S(2)}) collective-permute-start(f32[24,512]{1,0:T(8,128)S(1)} %message.1), channel_id=1, source_target_pairs={{1,0},{2,1},{3,2},{4,3},{5,4},{6,5},{7,6},{0,7},{9,8},{10,9},{11,1... | collective-permute-start | bytes 147464 | tf_op jit(solution)/shard_map/ppermute | solution.py:514

commit v5 on v4

--- a/solution.py
+++ b/solution.py
@@ -349,7 +349,7 @@
 
 
 def patch_kernel(
-    in_ref, line_ref, coef_ref, sent_ref, ihigh_ref, ilow_ref, out_ref, rhs_ref, dy_ref
+    in_ref, line_ref, coef_ref, sent_ref, ihigh_ref, ilow_ref, out_ref, rhs_ref, dy_ref, both_ref
 ):
     half, nz, width = in_ref.shape
     ny = width // 2
@@ -369,17 +369,31 @@
     )
     rhs_ref[...] = jnp.zeros_like(rhs_ref)
     for z in range(nz):
-        rhs_ref[2 * z : 2 * z + 1] = extra[z : z + 1]
-        rhs_ref[ny - 1 + 2 * z : ny + 2 * z] = last[z : z + 1]
-    solved = product((ihigh_ref[...], ilow_ref[...]), split(rhs_ref[...]), NT)
+        at = (width - 2 * z) % width
+        rhs_ref[at : at + 1] = extra[z : z + 1]
+        rhs_ref[ny - 1 - 2 * z : ny - 2 * z] = last[z : z + 1]
+    high, low = split(rhs_ref[...])
+    wide = lax.dot_general(
+        ihigh_ref[...], jnp.concatenate([high, low], axis=0), NT, preferred_element_type=jnp.float32
+    )
+    solved = wide[:, :width] + (
+        wide[:, width:]
+        + lax.dot_general(ilow_ref[...], high, NT, preferred_element_type=jnp.float32)
+    )
     lane = lax.broadcasted_iota(jnp.int32, (half, width), 1)
-    even = lane % 2 == 0
-    lower = ((lane < ny // 2) & even) | ((lane >= ny // 2) & (lane < ny + ny // 2) & ~even)
-    both = jnp.where(lower, solved[:half], pltpu.roll(solved[half:], ny, 1))
+    quarter = ny // 2
+    lower = ((lane < quarter) & (lane % 2 == 0)) | (
+        (lane >= quarter) & (lane < ny + quarter) & (lane % 2 == 1)
+    )
+    lower = lower | ((lane >= ny + quarter) & (lane % 2 == 0))
+    both_ref[...] = jnp.where(lower, solved[:half], pltpu.roll(solved[half:], ny, 1))
+    lane = lax.broadcasted_iota(jnp.int32, (nz, width), 1)
     ends = (lane % ny == 0) | (lane % ny == ny - 1)
-    for z in range(nz):
-        moved = pltpu.roll(both, width - 2 * z, 1) if z else both
-        out_ref[:, z, :] = in_ref[:, z, :] + jnp.where(ends, moved, 0.0)
+    for d in range(half):
+        moved = pltpu.roll(
+            jnp.broadcast_to(both_ref[d : d + 1], (nz, width)), 0, 1, stride=2, stride_axis=0
+        )
+        out_ref[d] = in_ref[d] + jnp.where(ends, moved, 0.0)
 
 
 def patch(tiles, line, coefs, sent, inv_high, inv_low):
@@ -393,6 +407,7 @@
         scratch_shapes=[
             pltpu.VMEM((width, nx), jnp.float32),
             pltpu.VMEM((16, nx), jnp.float32),
+            pltpu.VMEM((half, width), jnp.float32),
         ],
         compiler_params=pltpu.CompilerParams(vmem_limit_bytes=16 * 1024 * 1024),
         cost_estimate=pl.CostEstimate(
@@ -457,10 +472,10 @@
     sources, depth, width = in_ref.shape
     ny = width // 2
     copies = []
+    turned = jnp.transpose(in_ref[...], (1, 2, 0))
     for z in range(depth):
-        turned = in_ref[:, z, :].T
-        turned_ref[z, :, :sources] = turned[:ny]
-        turned_ref[z, :, sources:] = turned[ny:]
+        turned_ref[z, :, :sources] = turned[z, :ny]
+        turned_ref[z, :, sources:] = turned[z, ny:]
         copies.append(pltpu.make_async_copy(turned_ref.at[z], out_ref.at[z], sems.at[z]))
         copies[-1].start()
     for copy in copies:

time: 105 us -> 104 us (level)
  Pallas kernels: 12.9 us -> 11.8 us
where the time goes in v5:
time: 104 us; the launch traced here: 103 us
  blocking collectives  80.7 us (78%)
  Pallas kernels  11.8 us (11%)
  starting transfers between devices  9.49 us (9%)
    all_to_all x1, blocking collectives, shards(): lax.all_to_all(tiles, axes, split_axis=0, concat_axis=0, tiled=True)  43.4 us
    all_to_all x1, blocking collectives, shards(): lax.all_to_all(solved.reshape(planes.shape), axes, split_axis=0, concat_a...  37.3 us
    ppermute x1, starting transfers between devices, shards(): lax.ppermute(message(rows, coefs, z_inner, z_outer), 'gy', [((i + 1) % co...  5.47 us
    pallas_call x1, Pallas kernels, stencil(): pl.pallas_call(stencil_kernel, in_specs=[VMEM] * 7 + [HBM] * 2 + [VMEM] *...  3.68 us
    pallas_call x1, Pallas kernels, ionic(): pl.pallas_call(ionic_kernel, in_specs=[HBM] * 7, out_specs=[VMEM] * 8, ou...  3.35 us
    ppermute x1, starting transfers between devices, swaps(): lax.ppermute(inner, axis, both(0))  2.11 us
  transfers between devices with their start and end apart: 3, of which 0 were waited for; matrix products, arithmetic and copies ran while one was open for 0% of the time, Pallas kernels for 7%

profile of v5, /device:TPU:32, one launch (start us, length us, event | category | flops | bytes accessed | tf_op | source)
XLA Modules:
  0.0 102.8 jit_solution(14923392696272506154)
XLA Ops:
  0.6 1.0 faces.1
  1.6 1.9 %collective-permute-start = (f32[64,512]{1,0:T(8,128)S(1)}, f32[64,512]{1,0:T(8,128)S(1)}, u32[]{:S(2)}, u32[]{:S(2)}) collective-permute-start(f32[64,512]{1,0:T(8,128)S(1)} %get-tuple-element.27), channel_id=1, source_target_pairs={{8,16},{24,32},{40,48},{56,64},{72,80},{88,96},{104,112},{120,128}... | collective-permute-start | bytes 393224 | tf_op jit(solution)/shard_map/ppermute | solution.py:508
  3.6 2.1 %collective-permute-start.1 = (f32[64,512]{1,0:T(8,128)S(1)}, f32[64,512]{1,0:T(8,128)S(1)}, u32[]{:S(2)}, u32[]{:S(2)}) collective-permute-start(f32[64,512]{1,0:T(8,128)S(1)} %get-tuple-element.28), channel_id=1, source_target_pairs={{0,8},{16,24},{32,40},{48,56},{64,72},{80,88},{96,104},{112,120},{... | collective-permute-start | bytes 393224 | tf_op jit(solution)/shard_map/ppermute | solution.py:508
  5.7 3.4 %ionic.1 = (f32[8,64,512]{2,1,0:T(8,128)S(1)}, f32[8,64,512]{2,1,0:T(8,128)S(1)}, f32[24,512]{1,0:T(8,128)S(1)}, f32[3,8,512]{2,1,0:T(8,128)S(1)}, bf16[512,512]...) custom-call(f32[3,8]{1,0:T(4,128)} %bitcast.7, ...), custom_call_target="tpu_custom_call" | custom-call | flops 10485760 | bytes 7340032 | tf_op jit(solution)/shard_map/ionic/pallas_call | solution.py:133
  9.0 0.0 collective-permute-done.outer_ref
  9.0 0.0 collective-permute-done.1.inner_ref
  9.1 0.1 message.1
  9.2 5.5 %collective-permute-start.2 = (f32[24,512]{1,0:T(8,128)S(1)}, f32[24,512]{1,0:T(8,128)S(1)}, u32[]{:S(2)}, u32[]{:S(2)}) collective-permute-start(f32[24,512]{1,0:T(8,128)S(1)} %message.1), channel_id=1, source_target_pairs={{1,0},{2,1},{3,2},{4,3},{5,4},{6,5},{7,6},{0,7},{9,8},{10,9},{11,1... | collective-permute-start | bytes 147464 | tf_op jit(solution)/shard_map/ppermute | solution.py:529
  14.6 3.7 %stencil.1 = (f32[256,8,128]{2,1,0:T(8,128)S(1)}, f32[10,512]{1,0:T(8,128)S(1)}, bf16[256,256]{1,0:T(8,128)(2,1)S(1)}, bf16[256,256]{1,0:T(8,128)(2,1)S(1)}, bf1...) custom-call(f32[8,64,512]{2,1,0:T(8,128)S(1)} %get-tuple-element.25.pot, ...), custom_call_target="tpu_custom_call" | custom-call | flops 805306368 | bytes 8388608 | tf_op jit(solution)/shard_map/stencil/pallas_call | solution.py:320
  18.3 0.0 collective-permute-done.2.sent_ref
  18.3 0.9 patch.1
  19.3 43.4 %all_to_all.10 = f32[256,8,128]{2,1,0:T(8,128)S(1)} all-to-all(f32[256,8,128]{2,1,0:T(8,128)S(1)} %patch.1), channel_id=1, replica_groups=mesh['gz'=32,'gy'=8] {'gz','gy'}, dimensions={0} | all-to-all | bytes 2097152 | tf_op jit(solution)/shard_map/all_to_all | solution.py:537
  62.7 1.6 %plane_solve.1 = f32[32,8,8,128]{3,2,1,0:T(8,128)S(1)} custom-call(f32[32,8,8,128]{3,2,1,0:T(8,128)S(1)} %bitcast.4, bf16[256,256]{1,0:T(8,128)(2,1)S(1)} %get-tuple-element.41.zhigh_ref, bf16[256,256]{1,0:T(8,128)(2,1)S(1)} %get-tuple-element.42.zlow_ref, bf16[512,512]{1,0:T(8,128)(2,1)S(1)} %get-tuple-element.43.yhigh_ref, ...), custom_call_target="tpu_custom_call" | custom-call | flops 1207959552 | bytes 2097152 | tf_op jit(solution)/shard_map/plane_solve/pallas_call | solution.py:457
  64.3 37.3 %all_to_all.11.in_ref = f32[256,8,128]{2,1,0:T(8,128)S(1)} all-to-all(f32[256,8,128]{2,1,0:T(8,128)S(1)} %bitcast.5), channel_id=1, replica_groups=mesh['gz'=32,'gy'=8] {'gz','gy'}, dimensions={0} | all-to-all | bytes 2097152 | tf_op jit(solution)/shard_map/all_to_all | solution.py:540
  101.6 1.1 %unpack.1 = f32[8,64,512]{2,1,0:T(8,128)} custom-call(f32[256,8,128]{2,1,0:T(8,128)S(1)} %all_to_all.11.in_ref), custom_call_target="tpu_custom_call" | custom-call | bytes 2097152 | tf_op jit(solution)/shard_map/unpack/pallas_call | solution.py:488
Async XLA Ops:
  1.6 7.4 %collective-permute-start = (f32[64,512]{1,0:T(8,128)S(1)}, f32[64,512]{1,0:T(8,128)S(1)}, u32[]{:S(2)}, u32[]{:S(2)}) collective-permute-start(f32[64,512]{1,0:T(8,128)S(1)} %get-tuple-element.27), channel_id=1, source_target_pairs={{8,16},{24,32},{40,48},{56,64},{72,80},{88,96},{104,112},{120,128}... | collective-permute-start | bytes 393224 | tf_op jit(solution)/shard_map/ppermute | solution.py:508
  3.6 5.5 %collective-permute-start.1 = (f32[64,512]{1,0:T(8,128)S(1)}, f32[64,512]{1,0:T(8,128)S(1)}, u32[]{:S(2)}, u32[]{:S(2)}) collective-permute-start(f32[64,512]{1,0:T(8,128)S(1)} %get-tuple-element.28), channel_id=1, source_target_pairs={{0,8},{16,24},{32,40},{48,56},{64,72},{80,88},{96,104},{112,120},{... | collective-permute-start | bytes 393224 | tf_op jit(solution)/shard_map/ppermute | solution.py:508
  9.2 9.2 %collective-permute-start.2 = (f32[24,512]{1,0:T(8,128)S(1)}, f32[24,512]{1,0:T(8,128)S(1)}, u32[]{:S(2)}, u32[]{:S(2)}) collective-permute-start(f32[24,512]{1,0:T(8,128)S(1)} %message.1), channel_id=1, source_target_pairs={{1,0},{2,1},{3,2},{4,3},{5,4},{6,5},{7,6},{0,7},{9,8},{10,9},{11,1... | collective-permute-start | bytes 147464 | tf_op jit(solution)/shard_map/ppermute | solution.py:529

commit v6 on v5

--- a/solution.py
+++ b/solution.py
@@ -117,7 +117,9 @@
             keep_slow = jnp.where(active, decay(wclose_tau), decay(wopen_tau))
             nfast_ref[rows] = jnp.where(living, target + (v - target) * keep_fast, v)
             nslow_ref[rows] = jnp.where(living, target + (w - target) * keep_slow, w)
-        for k, line in enumerate((potc_ref[z, 0:1], potc_ref[z, 1:2], exc_ref[z, 0:1])):
+        for k, line in enumerate(
+            (potc_ref[z, ny - 1 :], potc_ref[z, ny - 2 : ny - 1], exc_ref[z, ny - 1 :])
+        ):
             rows_ref[k * nz + z : k * nz + z + 1] = line
     for copy in extra:
         copy.wait()
@@ -208,21 +210,23 @@
 def message_kernel(rows_ref, coef_ref, inner_ref, outer_ref, out_ref, pad_ref):
     nz = rows_ref.shape[0] // 3
     pads = nz + 2
+    ny = inner_ref.shape[0]
+    block = slice(coef_ref.shape[1] - 1, coef_ref.shape[1])
     odd = lax.axis_index("gz") % 2
     for k in range(2):
-        row = slice(k, k + 1)
+        row = slice(ny - 1 - k, ny - k)
         below, above = ordered(odd, inner_ref[row], outer_ref[row])
         pad_ref[k, 0:1] = below
         pad_ref[k, 1 : nz + 1] = rows_ref[k * nz : (k + 1) * nz]
         pad_ref[k, nz + 1 : pads] = above
     out_ref[0:nz] = rows_ref[2 * nz :] + (
-        coef_ref[0, 0:1] * lane_difference(pad_ref[1, 1 : nz + 1])
-        + coef_ref[1, 0:1] * lane_difference(pad_ref[0, 2:pads] - pad_ref[0, 0:nz])
-        + coef_ref[2, 0:1] * (pad_ref[1, 2:pads] - pad_ref[1, 0:nz])
+        coef_ref[1, block] * lane_difference(pad_ref[0, 2:pads] - pad_ref[0, 0:nz])
+        - coef_ref[0, block] * lane_difference(pad_ref[1, 1 : nz + 1])
+        - coef_ref[2, block] * (pad_ref[1, 2:pads] - pad_ref[1, 0:nz])
     )
     out_ref[nz : nz + pads] = pad_ref[0, 0:pads]
-    out_ref[nz + pads : nz + pads + 1] = coef_ref[0, 0:1]
-    out_ref[nz + pads + 1 : nz + pads + 2] = coef_ref[2, 0:1]
+    out_ref[nz + pads : nz + pads + 1] = coef_ref[0, block]
+    out_ref[nz + pads + 1 : nz + pads + 2] = coef_ref[2, block]
     rest = out_ref.shape[0] - (nz + pads + 2)
     out_ref[nz + pads + 2 :] = jnp.zeros((rest, out_ref.shape[1]), jnp.float32)
 
@@ -266,7 +270,7 @@
         pad_ref[z, 7:8] = nothing
         pad_ref[z, 8 + ny : 9 + ny] = nothing
         dy_ref[z] = pad_ref[z, 9 : 9 + ny] - pad_ref[z, 7 : 7 + ny]
-        line_ref[z : z + 1] = plane[ny - 1 :]
+        line_ref[z : z + 1] = plane[0:1]
     row = lax.broadcasted_iota(jnp.int32, (8, nx), 0)
     first = lax.broadcasted_iota(jnp.int32, (half, 2 * ny), 1) < ny
     matrix = ihigh_ref[...], ilow_ref[...]
@@ -287,7 +291,7 @@
                     + coef_ref[2, b : b + 1] * mixed_yz
                 )
             )
-        parts[0] = jnp.where(row == 0, 0.0, parts[0])
+        parts[-1] = jnp.where(row == 7, 0.0, parts[-1])
         for b in range(0, blocks, 2):
             rows = slice(z * ny + 8 * b, z * ny + 8 * b + 16)
             high_ref[rows], low_ref[rows] = split(jnp.concatenate(parts[b : b + 2], axis=0))
@@ -303,11 +307,10 @@
     for copy in loads:
         copy.wait()
     zhigh_ref[...], zlow_ref[...] = split(invz_v[...])
-    width = invy_v.shape[1]
     invy = invy_v[...]
     column = lax.broadcasted_iota(jnp.int32, invy.shape, 1)
     yhigh_ref[...], ylow_ref[...] = split(
-        jnp.where(column % ny == 0, pltpu.roll(invy, width - ny, 1), invy)
+        jnp.where(column % ny == ny - 1, pltpu.roll(invy, ny, 1), invy)
     )
     for copy in stores:
         copy.wait()
@@ -354,24 +357,23 @@
     half, nz, width = in_ref.shape
     ny = width // 2
     pads = nz + 2
-    keep = jnp.where(lax.axis_index("gy") == lax.axis_size("gy") - 1, 0.0, 1.0)
+    keep = jnp.where(lax.axis_index("gy") == 0, 0.0, 1.0)
     inside = slice(1, nz + 1)
-    row = slice(coef_ref.shape[1] - 1, coef_ref.shape[1])
-    dy_ref[0:pads] = sent_ref[nz : nz + pads] * keep
-    last = coef_ref[0, row] * lane_difference(dy_ref[inside]) + coef_ref[2, row] * (
+    dy_ref[0:pads] = sent_ref[nz : nz + pads] * -keep
+    first = coef_ref[0, 0:1] * lane_difference(dy_ref[inside]) + coef_ref[2, 0:1] * (
         dy_ref[2:pads] - dy_ref[0:nz]
     )
     dy_ref[0:pads] = line_ref[...] * keep
     end = nz + pads
-    extra = sent_ref[0:nz] - (
+    extra = sent_ref[0:nz] + (
         sent_ref[end : end + 1] * lane_difference(dy_ref[inside])
         + sent_ref[end + 1 : end + 2] * (dy_ref[2:pads] - dy_ref[0:nz])
     )
     rhs_ref[...] = jnp.zeros_like(rhs_ref)
     for z in range(nz):
         at = (width - 2 * z) % width
-        rhs_ref[at : at + 1] = extra[z : z + 1]
-        rhs_ref[ny - 1 - 2 * z : ny - 2 * z] = last[z : z + 1]
+        rhs_ref[at : at + 1] = first[z : z + 1]
+        rhs_ref[ny - 1 - 2 * z : ny - 2 * z] = extra[z : z + 1]
     high, low = split(rhs_ref[...])
     wide = lax.dot_general(
         ihigh_ref[...], jnp.concatenate([high, low], axis=0), NT, preferred_element_type=jnp.float32
@@ -527,7 +529,7 @@
     z_outer, z_inner, rows, coefs = lax.optimization_barrier((z_outer, z_inner, rows, coefs))
     count = lax.axis_size("gy")
     sent = lax.ppermute(
-        message(rows, coefs, z_inner, z_outer), "gy", [((i + 1) % count, i) for i in range(count)]
+        message(rows, coefs, z_inner, z_outer), "gy", [(i, (i + 1) % count) for i in range(count)]
     )
     tiles, line, *matrices, new_fast, new_slow = stencil(
         held, excited, coefs, z_inner, z_outer, inv_high, inv_low, inverse_z, inverse_y, *gates

time: 104 us -> 102 us (0.981)
  starting transfers between devices: 9.49 us -> 7.3 us
    ppermute x1, starting transfers between devices: 5.47 us -> 3.27 us  [shards(): lax.ppermute(message(rows, coefs, z_inner, z_outer), 'gy', [(i, (i + 1) %...]
  transfers between devices with their start and end apart: 3 -> 3, of which waited for: 0 -> 1; matrix products, arithmetic and copies ran while one was open for 0% -> 0% of each run, Pallas kernels for 7% -> 7%
where the time goes in v6:
time: 102 us; the launch traced here: 101 us
  blocking collectives  80.3 us (79%)
  Pallas kernels  11.8 us (12%)
  starting transfers between devices  7.3 us (7%)
    all_to_all x1, blocking collectives, shards(): lax.all_to_all(tiles, axes, split_axis=0, concat_axis=0, tiled=True)  43 us
    all_to_all x1, blocking collectives, shards(): lax.all_to_all(solved.reshape(planes.shape), axes, split_axis=0, concat_a...  37.3 us
    pallas_call x1, Pallas kernels, stencil(): pl.pallas_call(stencil_kernel, in_specs=[VMEM] * 7 + [HBM] * 2 + [VMEM] *...  3.68 us
    pallas_call x1, Pallas kernels, ionic(): pl.pallas_call(ionic_kernel, in_specs=[HBM] * 7, out_specs=[VMEM] * 8, ou...  3.36 us
    ppermute x1, starting transfers between devices, shards(): lax.ppermute(message(rows, coefs, z_inner, z_outer), 'gy', [(i, (i + 1) %...  3.27 us
    ppermute x1, starting transfers between devices, swaps(): lax.ppermute(inner, axis, both(0))  2.11 us
  transfers between devices with their start and end apart: 3, of which 1 were waited for; matrix products, arithmetic and copies ran while one was open for 0% of the time, Pallas kernels for 7%

profile of v6, /device:TPU:32, one launch (start us, length us, event | category | flops | bytes accessed | tf_op | source)
XLA Modules:
  0.0 100.9 jit_solution(14869213675580910099)
XLA Ops:
  0.6 1.0 faces.1
  1.6 1.9 %collective-permute-start = (f32[64,512]{1,0:T(8,128)S(1)}, f32[64,512]{1,0:T(8,128)S(1)}, u32[]{:S(2)}, u32[]{:S(2)}) collective-permute-start(f32[64,512]{1,0:T(8,128)S(1)} %get-tuple-element.27), channel_id=1, source_target_pairs={{8,16},{24,32},{40,48},{56,64},{72,80},{88,96},{104,112},{120,128}... | collective-permute-start | bytes 393224 | tf_op jit(solution)/shard_map/ppermute | solution.py:510
  3.6 2.1 %collective-permute-start.1 = (f32[64,512]{1,0:T(8,128)S(1)}, f32[64,512]{1,0:T(8,128)S(1)}, u32[]{:S(2)}, u32[]{:S(2)}) collective-permute-start(f32[64,512]{1,0:T(8,128)S(1)} %get-tuple-element.28), channel_id=1, source_target_pairs={{0,8},{16,24},{32,40},{48,56},{64,72},{80,88},{96,104},{112,120},{... | collective-permute-start | bytes 393224 | tf_op jit(solution)/shard_map/ppermute | solution.py:510
  5.7 3.4 %ionic.1 = (f32[8,64,512]{2,1,0:T(8,128)S(1)}, f32[8,64,512]{2,1,0:T(8,128)S(1)}, f32[24,512]{1,0:T(8,128)S(1)}, f32[3,8,512]{2,1,0:T(8,128)S(1)}, bf16[512,512]...) custom-call(f32[3,8]{1,0:T(4,128)} %bitcast.7, ...), custom_call_target="tpu_custom_call" | custom-call | flops 10485760 | bytes 7340032 | tf_op jit(solution)/shard_map/ionic/pallas_call | solution.py:135
  9.0 0.0 collective-permute-done.outer_ref
  9.0 0.0 collective-permute-done.1.inner_ref
  9.1 0.1 message.1
  9.2 3.3 %collective-permute-start.2 = (f32[24,512]{1,0:T(8,128)S(1)}, f32[24,512]{1,0:T(8,128)S(1)}, u32[]{:S(2)}, u32[]{:S(2)}) collective-permute-start(f32[24,512]{1,0:T(8,128)S(1)} %message.1), channel_id=1, source_target_pairs={{0,1},{1,2},{2,3},{3,4},{4,5},{5,6},{6,7},{7,0},{8,9},{9,10},{10,1... | collective-permute-start | bytes 147464 | tf_op jit(solution)/shard_map/ppermute | solution.py:531
  12.4 3.7 %stencil.1 = (f32[256,8,128]{2,1,0:T(8,128)S(1)}, f32[10,512]{1,0:T(8,128)S(1)}, bf16[256,256]{1,0:T(8,128)(2,1)S(1)}, bf16[256,256]{1,0:T(8,128)(2,1)S(1)}, bf1...) custom-call(f32[8,64,512]{2,1,0:T(8,128)S(1)} %get-tuple-element.25.pot, ...), custom_call_target="tpu_custom_call" | custom-call | flops 805306368 | bytes 8388608 | tf_op jit(solution)/shard_map/stencil/pallas_call | solution.py:323
  16.1 0.8 collective-permute-done.2.sent_ref
  17.0 0.9 patch.1
  17.9 43.0 %all_to_all.10 = f32[256,8,128]{2,1,0:T(8,128)S(1)} all-to-all(f32[256,8,128]{2,1,0:T(8,128)S(1)} %patch.1), channel_id=1, replica_groups=mesh['gz'=32,'gy'=8] {'gz','gy'}, dimensions={0} | all-to-all | bytes 2097152 | tf_op jit(solution)/shard_map/all_to_all | solution.py:539
  60.8 1.6 %plane_solve.1 = f32[32,8,8,128]{3,2,1,0:T(8,128)S(1)} custom-call(f32[32,8,8,128]{3,2,1,0:T(8,128)S(1)} %bitcast.4, bf16[256,256]{1,0:T(8,128)(2,1)S(1)} %get-tuple-element.41.zhigh_ref, bf16[256,256]{1,0:T(8,128)(2,1)S(1)} %get-tuple-element.42.zlow_ref, bf16[512,512]{1,0:T(8,128)(2,1)S(1)} %get-tuple-element.43.yhigh_ref, ...), custom_call_target="tpu_custom_call" | custom-call | flops 1207959552 | bytes 2097152 | tf_op jit(solution)/shard_map/plane_solve/pallas_call | solution.py:459
  62.5 37.3 %all_to_all.11.in_ref = f32[256,8,128]{2,1,0:T(8,128)S(1)} all-to-all(f32[256,8,128]{2,1,0:T(8,128)S(1)} %bitcast.5), channel_id=1, replica_groups=mesh['gz'=32,'gy'=8] {'gz','gy'}, dimensions={0} | all-to-all | bytes 2097152 | tf_op jit(solution)/shard_map/all_to_all | solution.py:542
  99.8 1.1 %unpack.1 = f32[8,64,512]{2,1,0:T(8,128)} custom-call(f32[256,8,128]{2,1,0:T(8,128)S(1)} %all_to_all.11.in_ref), custom_call_target="tpu_custom_call" | custom-call | bytes 2097152 | tf_op jit(solution)/shard_map/unpack/pallas_call | solution.py:490
Async XLA Ops:
  1.6 7.4 %collective-permute-start = (f32[64,512]{1,0:T(8,128)S(1)}, f32[64,512]{1,0:T(8,128)S(1)}, u32[]{:S(2)}, u32[]{:S(2)}) collective-permute-start(f32[64,512]{1,0:T(8,128)S(1)} %get-tuple-element.27), channel_id=1, source_target_pairs={{8,16},{24,32},{40,48},{56,64},{72,80},{88,96},{104,112},{120,128}... | collective-permute-start | bytes 393224 | tf_op jit(solution)/shard_map/ppermute | solution.py:510
  3.6 5.5 %collective-permute-start.1 = (f32[64,512]{1,0:T(8,128)S(1)}, f32[64,512]{1,0:T(8,128)S(1)}, u32[]{:S(2)}, u32[]{:S(2)}) collective-permute-start(f32[64,512]{1,0:T(8,128)S(1)} %get-tuple-element.28), channel_id=1, source_target_pairs={{0,8},{16,24},{32,40},{48,56},{64,72},{80,88},{96,104},{112,120},{... | collective-permute-start | bytes 393224 | tf_op jit(solution)/shard_map/ppermute | solution.py:510
  9.2 7.8 %collective-permute-start.2 = (f32[24,512]{1,0:T(8,128)S(1)}, f32[24,512]{1,0:T(8,128)S(1)}, u32[]{:S(2)}, u32[]{:S(2)}) collective-permute-start(f32[24,512]{1,0:T(8,128)S(1)} %message.1), channel_id=1, source_target_pairs={{0,1},{1,2},{2,3},{3,4},{4,5},{5,6},{6,7},{7,0},{8,9},{9,10},{10,1... | collective-permute-start | bytes 147464 | tf_op jit(solution)/shard_map/ppermute | solution.py:531

commit v7 on v6

--- a/solution.py
+++ b/solution.py
@@ -219,16 +219,18 @@
         pad_ref[k, 0:1] = below
         pad_ref[k, 1 : nz + 1] = rows_ref[k * nz : (k + 1) * nz]
         pad_ref[k, nz + 1 : pads] = above
-    out_ref[0:nz] = rows_ref[2 * nz :] + (
+    partial = rows_ref[2 * nz :] + (
         coef_ref[1, block] * lane_difference(pad_ref[0, 2:pads] - pad_ref[0, 0:nz])
         - coef_ref[0, block] * lane_difference(pad_ref[1, 1 : nz + 1])
         - coef_ref[2, block] * (pad_ref[1, 2:pads] - pad_ref[1, 0:nz])
     )
-    out_ref[nz : nz + pads] = pad_ref[0, 0:pads]
-    out_ref[nz + pads : nz + pads + 1] = coef_ref[0, block]
-    out_ref[nz + pads + 1 : nz + pads + 2] = coef_ref[2, block]
-    rest = out_ref.shape[0] - (nz + pads + 2)
-    out_ref[nz + pads + 2 :] = jnp.zeros((rest, out_ref.shape[1]), jnp.float32)
+    lines = nz + pads + 2
+    parts = ((0, partial), (nz, pad_ref[0, 0:pads]))
+    parts += ((nz + pads, coef_ref[0, block]), (nz + pads + 1, coef_ref[2, block]))
+    for start, part in parts:
+        for k in range(part.shape[1] // 128):
+            at = k * lines + start
+            out_ref[at : at + part.shape[0]] = part[:, 128 * k : 128 * (k + 1)]
 
 
 def message(rows, coefs, inner, outer):
@@ -237,7 +239,7 @@
         message_kernel,
         in_specs=[VMEM] * 4,
         out_specs=VMEM,
-        out_shape=pltpu.VMEM((3 * nz, nx), jnp.float32),
+        out_shape=pltpu.VMEM(((2 * nz + 4) * nx // 128, 128), jnp.float32),
         scratch_shapes=[pltpu.VMEM((2, 16, nx), jnp.float32)],
         compiler_params=pltpu.CompilerParams(vmem_limit_bytes=4 * 1024 * 1024),
         name="message",
@@ -352,12 +354,16 @@
 
 
 def patch_kernel(
-    in_ref, line_ref, coef_ref, sent_ref, ihigh_ref, ilow_ref, out_ref, rhs_ref, dy_ref, both_ref
+    in_ref, line_ref, coef_ref, packed_ref, ihigh_ref, ilow_ref,
+    out_ref, rhs_ref, dy_ref, both_ref, sent_ref,
 ):
     half, nz, width = in_ref.shape
     ny = width // 2
     pads = nz + 2
     keep = jnp.where(lax.axis_index("gy") == 0, 0.0, 1.0)
+    lines = nz + pads + 2
+    for k in range(packed_ref.shape[0] // lines):
+        sent_ref[0:lines, 128 * k : 128 * (k + 1)] = packed_ref[k * lines : (k + 1) * lines]
     inside = slice(1, nz + 1)
     dy_ref[0:pads] = sent_ref[nz : nz + pads] * -keep
     first = coef_ref[0, 0:1] * lane_difference(dy_ref[inside]) + coef_ref[2, 0:1] * (
@@ -410,6 +416,7 @@
             pltpu.VMEM((width, nx), jnp.float32),
             pltpu.VMEM((16, nx), jnp.float32),
             pltpu.VMEM((half, width), jnp.float32),
+            pltpu.VMEM((3 * nz, nx), jnp.float32),
         ],
         compiler_params=pltpu.CompilerParams(vmem_limit_bytes=16 * 1024 * 1024),
         cost_estimate=pl.CostEstimate(

time: 102 us -> 102 us (level)
  no operation moved by 1% of the time
where the time goes in v7:
time: 102 us; the launch traced here: 101 us
  blocking collectives  80.3 us (79%)
  Pallas kernels  11.8 us (12%)
  starting transfers between devices  7.3 us (7%)
    all_to_all x1, blocking collectives, shards(): lax.all_to_all(tiles, axes, split_axis=0, concat_axis=0, tiled=True)  43 us
    all_to_all x1, blocking collectives, shards(): lax.all_to_all(solved.reshape(planes.shape), axes, split_axis=0, concat_a...  37.3 us
    pallas_call x1, Pallas kernels, stencil(): pl.pallas_call(stencil_kernel, in_specs=[VMEM] * 7 + [HBM] * 2 + [VMEM] *...  3.68 us
    pallas_call x1, Pallas kernels, ionic(): pl.pallas_call(ionic_kernel, in_specs=[HBM] * 7, out_specs=[VMEM] * 8, ou...  3.36 us
    ppermute x1, starting transfers between devices, shards(): lax.ppermute(message(rows, coefs, z_inner, z_outer), 'gy', [(i, (i + 1) %...  3.27 us
    ppermute x1, starting transfers between devices, swaps(): lax.ppermute(inner, axis, both(0))  2.11 us
  transfers between devices with their start and end apart: 3, of which 1 were waited for; matrix products, arithmetic and copies ran while one was open for 0% of the time, Pallas kernels for 7%

profile of v7, /device:TPU:32, one launch (start us, length us, event | category | flops | bytes accessed | tf_op | source)
XLA Modules:
  0.0 100.8 jit_solution(2307712698315050572)
XLA Ops:
  0.6 1.0 faces.1
  1.6 1.9 %collective-permute-start = (f32[64,512]{1,0:T(8,128)S(1)}, f32[64,512]{1,0:T(8,128)S(1)}, u32[]{:S(2)}, u32[]{:S(2)}) collective-permute-start(f32[64,512]{1,0:T(8,128)S(1)} %get-tuple-element.27), channel_id=1, source_target_pairs={{8,16},{24,32},{40,48},{56,64},{72,80},{88,96},{104,112},{120,128}... | collective-permute-start | bytes 393224 | tf_op jit(solution)/shard_map/ppermute | solution.py:517
  3.6 2.1 %collective-permute-start.1 = (f32[64,512]{1,0:T(8,128)S(1)}, f32[64,512]{1,0:T(8,128)S(1)}, u32[]{:S(2)}, u32[]{:S(2)}) collective-permute-start(f32[64,512]{1,0:T(8,128)S(1)} %get-tuple-element.28), channel_id=1, source_target_pairs={{0,8},{16,24},{32,40},{48,56},{64,72},{80,88},{96,104},{112,120},{... | collective-permute-start | bytes 393224 | tf_op jit(solution)/shard_map/ppermute | solution.py:517
  5.7 3.4 %ionic.1 = (f32[8,64,512]{2,1,0:T(8,128)S(1)}, f32[8,64,512]{2,1,0:T(8,128)S(1)}, f32[24,512]{1,0:T(8,128)S(1)}, f32[3,8,512]{2,1,0:T(8,128)S(1)}, bf16[512,512]...) custom-call(f32[3,8]{1,0:T(4,128)} %bitcast.7, ...), custom_call_target="tpu_custom_call" | custom-call | flops 10485760 | bytes 7340032 | tf_op jit(solution)/shard_map/ionic/pallas_call | solution.py:135
  9.0 0.0 collective-permute-done.outer_ref
  9.0 0.0 collective-permute-done.1.inner_ref
  9.1 0.1 message.1
  9.2 3.3 %collective-permute-start.2 = (f32[80,128]{1,0:T(8,128)S(1)}, f32[80,128]{1,0:T(8,128)S(1)}, u32[]{:S(2)}, u32[]{:S(2)}) collective-permute-start(f32[80,128]{1,0:T(8,128)S(1)} %message.1), channel_id=1, source_target_pairs={{0,1},{1,2},{2,3},{3,4},{4,5},{5,6},{6,7},{7,0},{8,9},{9,10},{10,1... | collective-permute-start | bytes 122888 | tf_op jit(solution)/shard_map/ppermute | solution.py:538
  12.4 3.7 %stencil.1 = (f32[256,8,128]{2,1,0:T(8,128)S(1)}, f32[10,512]{1,0:T(8,128)S(1)}, bf16[256,256]{1,0:T(8,128)(2,1)S(1)}, bf16[256,256]{1,0:T(8,128)(2,1)S(1)}, bf1...) custom-call(f32[8,64,512]{2,1,0:T(8,128)S(1)} %get-tuple-element.25.pot, ...), custom_call_target="tpu_custom_call" | custom-call | flops 805306368 | bytes 8388608 | tf_op jit(solution)/shard_map/stencil/pallas_call | solution.py:325
  16.1 0.7 collective-permute-done.2.packed_ref
  16.9 0.9 patch.1
  17.8 43.0 %all_to_all.10 = f32[256,8,128]{2,1,0:T(8,128)S(1)} all-to-all(f32[256,8,128]{2,1,0:T(8,128)S(1)} %patch.1), channel_id=1, replica_groups=mesh['gz'=32,'gy'=8] {'gz','gy'}, dimensions={0} | all-to-all | bytes 2097152 | tf_op jit(solution)/shard_map/all_to_all | solution.py:546
  60.7 1.6 %plane_solve.1 = f32[32,8,8,128]{3,2,1,0:T(8,128)S(1)} custom-call(f32[32,8,8,128]{3,2,1,0:T(8,128)S(1)} %bitcast.4, bf16[256,256]{1,0:T(8,128)(2,1)S(1)} %get-tuple-element.41.zhigh_ref, bf16[256,256]{1,0:T(8,128)(2,1)S(1)} %get-tuple-element.42.zlow_ref, bf16[512,512]{1,0:T(8,128)(2,1)S(1)} %get-tuple-element.43.yhigh_ref, ...), custom_call_target="tpu_custom_call" | custom-call | flops 1207959552 | bytes 2097152 | tf_op jit(solution)/shard_map/plane_solve/pallas_call | solution.py:466
  62.4 37.3 %all_to_all.11.in_ref = f32[256,8,128]{2,1,0:T(8,128)S(1)} all-to-all(f32[256,8,128]{2,1,0:T(8,128)S(1)} %bitcast.5), channel_id=1, replica_groups=mesh['gz'=32,'gy'=8] {'gz','gy'}, dimensions={0} | all-to-all | bytes 2097152 | tf_op jit(solution)/shard_map/all_to_all | solution.py:549
  99.7 1.1 %unpack.1 = f32[8,64,512]{2,1,0:T(8,128)} custom-call(f32[256,8,128]{2,1,0:T(8,128)S(1)} %all_to_all.11.in_ref), custom_call_target="tpu_custom_call" | custom-call | bytes 2097152 | tf_op jit(solution)/shard_map/unpack/pallas_call | solution.py:497
Async XLA Ops:
  1.6 7.4 %collective-permute-start = (f32[64,512]{1,0:T(8,128)S(1)}, f32[64,512]{1,0:T(8,128)S(1)}, u32[]{:S(2)}, u32[]{:S(2)}) collective-permute-start(f32[64,512]{1,0:T(8,128)S(1)} %get-tuple-element.27), channel_id=1, source_target_pairs={{8,16},{24,32},{40,48},{56,64},{72,80},{88,96},{104,112},{120,128}... | collective-permute-start | bytes 393224 | tf_op jit(solution)/shard_map/ppermute | solution.py:517
  3.6 5.5 %collective-permute-start.1 = (f32[64,512]{1,0:T(8,128)S(1)}, f32[64,512]{1,0:T(8,128)S(1)}, u32[]{:S(2)}, u32[]{:S(2)}) collective-permute-start(f32[64,512]{1,0:T(8,128)S(1)} %get-tuple-element.28), channel_id=1, source_target_pairs={{0,8},{16,24},{32,40},{48,56},{64,72},{80,88},{96,104},{112,120},{... | collective-permute-start | bytes 393224 | tf_op jit(solution)/shard_map/ppermute | solution.py:517
  9.2 7.7 %collective-permute-start.2 = (f32[80,128]{1,0:T(8,128)S(1)}, f32[80,128]{1,0:T(8,128)S(1)}, u32[]{:S(2)}, u32[]{:S(2)}) collective-permute-start(f32[80,128]{1,0:T(8,128)S(1)} %message.1), channel_id=1, source_target_pairs={{0,1},{1,2},{2,3},{3,4},{4,5},{5,6},{6,7},{7,0},{8,9},{9,10},{10,1... | collective-permute-start | bytes 122888 | tf_op jit(solution)/shard_map/ppermute | solution.py:538
